TPU v7x, 32 devices: a whole 2x2x4 slice. The times are simulated.
32 devices in a mesh: grp: 8 (over z, x), sub: 4 (over y, core).
Axes of the slice: x: 2, y: 2, z: 4, core: 2. Of those that a mesh axis runs over, the one named last changes fastest.
Arguments:
- field: float32 [128, 2, 16, 256], P(('grp', 'sub')), may hold values from -6 to 6
- source: float32 [128, 2, 16, 256], P(('grp', 'sub')), may hold values from -6 to 6
- patch_of_slot: int32 [128], P(('grp', 'sub')), may hold values from -1 to 11, as said below
- neighbour: int32 [128, 6], P(('grp', 'sub')), may hold values from -1 to 15, as said below
- wave_index: int32 [128], P(('grp', 'sub')), may hold values from 0 to 15
- wave_table: float32 [16], replicated, may hold values from 0.02 to 0.2
Outputs:
- corrected: float32 [128, 2, 16, 256], P(('grp', 'sub'))
Inputs may be any that keep to these rules, and one draw needn't show every extreme that they name: `patch_of_slot`: in each slab every patch 0 to 11 is held by exactly one slot; each device holds 2 to 4 patches in its first slots, the rest -1; in every slab some device holds 4 and some 2. `neighbour`: consistent with patch_of_slot and the slab grid: -1 exactly for empty slots, for faces on the grid's boundary.
All inputs are finite; a program needn't handle non-finite values.
Results may differ from a plain program's by a relative error of at most 0.0003.
Values sent between devices are 32-bit elements; how exact they have to be, the bound alone decides.
A program may use at most 64 MiB of HBM per device.

v0:
```python
import jax
import jax.numpy as jnp
from jax import lax
from jax.sharding import PartitionSpec as P

PZ = 4
CITER = 3


omega_fine = 0.7
omega_coarse = 0.6
shift_imag = 0.5


def padded_2(cells, sides, width):
    for axis, dim in sides:
        count = lax.axis_size(axis)
        ends = count - 1
        head = lax.slice_in_dim(cells, 0, width, axis=dim)
        tail = lax.slice_in_dim(cells, cells.shape[dim] - width, cells.shape[dim], axis=dim)
        cells = jnp.concatenate(
            [
                lax.ppermute(tail, axis, [(i, (i + 1) % count) for i in range(ends)]),
                cells,
                lax.ppermute(head, axis, [((i + 1) % count, i) for i in range(ends)]),
            ],
            axis=dim,
        )
    return cells


def faces_of(cubes):
    slot_count = cubes.shape[0]
    edge = cubes.shape[2]
    layers = [
        cubes[:, :, 0],
        cubes[:, :, -1],
        cubes[:, :, :, 0],
        cubes[:, :, :, -1],
        cubes[:, :, :, :, 0],
        cubes[:, :, :, :, -1],
    ]
    return jnp.stack([layer.reshape(slot_count, 2, edge * edge) for layer in layers], 1)


def neighbour_sum(cubes, ghosts):
    slot_count = cubes.shape[0]
    edge = cubes.shape[2]
    ghost_sheets = ghosts.reshape(slot_count, 6, 2, edge, edge)
    total = jnp.concatenate([ghost_sheets[:, 0][:, :, None], cubes[:, :, :-1]], 2)
    total = total + jnp.concatenate([cubes[:, :, 1:], ghost_sheets[:, 1][:, :, None]], 2)
    total = total + jnp.concatenate([ghost_sheets[:, 2][:, :, :, None], cubes[:, :, :, :-1]], 3)
    total = total + jnp.concatenate([cubes[:, :, :, 1:], ghost_sheets[:, 3][:, :, :, None]], 3)
    total = total + jnp.concatenate([ghost_sheets[:, 4][..., None], cubes[..., :-1]], 4)
    total = total + jnp.concatenate([cubes[..., 1:], ghost_sheets[:, 5][..., None]], 4)
    return total


def residual_of(cubes, rights, ghosts, wave_sq):
    beside_all = neighbour_sum(cubes, ghosts)
    scale = wave_sq[:, None, None, None]
    real_part = cubes[:, 0]
    imag_part = cubes[:, 1]
    apply_real = 6.0 * real_part - beside_all[:, 0] - scale * (real_part - shift_imag * imag_part)
    apply_imag = 6.0 * imag_part - beside_all[:, 1] - scale * (imag_part + shift_imag * real_part)
    return jnp.stack([rights[:, 0] - apply_real, rights[:, 1] - apply_imag], 1)


def divide_diag(values, real_diag, imag_diag, channel_axis):
    denom = real_diag * real_diag + imag_diag * imag_diag
    first = jnp.take(values, 0, axis=channel_axis)
    second = jnp.take(values, 1, axis=channel_axis)
    out_real = (first * real_diag - second * imag_diag) / denom
    out_imag = (first * imag_diag + second * real_diag) / denom
    return jnp.stack([out_real, out_imag], channel_axis)


def smooth_step(cubes, resid, wave_sq):
    scale = wave_sq[:, None, None, None]
    step_value = divide_diag(resid, 6.0 - scale, shift_imag * scale, 1)
    return cubes + omega_fine * step_value


def restrict(resid):
    slot_count = resid.shape[0]
    edge = resid.shape[2]
    small = edge // 4
    blocks = resid.reshape(slot_count, 2, small, 4, small, 4, small, 4)
    return jnp.mean(blocks, axis=(3, 5, 7)).reshape(slot_count, 2 * small * small * small)


def coarse_residual(padded_x, coarse_rhs, coarse_wave):
    current = padded_x[:, 1:-1]
    beside_all = padded_x[:, :-2] + padded_x[:, 2:]
    ypad = jnp.pad(current, ((0, 0), (0, 0), (1, 1), (0, 0)))
    beside_all = beside_all + ypad[:, :, :-2] + ypad[:, :, 2:]
    zpad = jnp.pad(current, ((0, 0), (0, 0), (0, 0), (1, 1)))
    beside_all = beside_all + zpad[..., :-2] + zpad[..., 2:]
    real_part = current[0]
    imag_part = current[1]
    apply_real = (6.0 * real_part - beside_all[0]) / 16.0 - coarse_wave * (
        real_part - shift_imag * imag_part
    )
    apply_imag = (6.0 * imag_part - beside_all[1]) / 16.0 - coarse_wave * (
        imag_part + shift_imag * real_part
    )
    return jnp.stack([coarse_rhs[0] - apply_real, coarse_rhs[1] - apply_imag], 0)


def coarse_divide(values, coarse_wave):
    return divide_diag(values, 6.0 / 16.0 - coarse_wave, shift_imag * coarse_wave, 0)


def ghost_layers(cubes, links):
    own_faces = faces_of(cubes)
    table = lax.all_gather(own_faces, "sub", axis=0, tiled=True)
    rims = jnp.stack([table[:, 0], table[:, 1]], 0)
    extended = padded_2(rims, (("grp", 0),), 1)
    lower = extended[0]
    upper = extended[3]
    inside = jnp.concatenate([table[:, 3:4], table[:, 2:3], table[:, 5:6], table[:, 4:5]], 1)
    candidate = jnp.concatenate([lower[:, None], upper[:, None], inside], 1)
    safe_links = jnp.maximum(links, 0)
    picked = candidate[safe_links, jnp.arange(6)[None, :]]
    return jnp.where((links >= 0)[:, :, None, None], picked, 0.0)


def body(field, source, patch_of_slot, neighbour, wave_index, wave_table):
    slot_count = field.shape[0]
    edge = field.shape[2]
    small = edge // 4
    patch_total = 3 * lax.axis_size("sub")
    rows_y = patch_total // PZ
    cubes = field.reshape(slot_count, 2, edge, edge, edge)
    rights = source.reshape(slot_count, 2, edge, edge, edge)
    selector_wave = (wave_index[:, None] == jnp.arange(wave_table.shape[0])[None, :]).astype(
        jnp.float32
    )
    wave_sq = jnp.sum(selector_wave * wave_table[None, :], 1)
    for sweep_index in range(2):
        ghosts = ghost_layers(cubes, neighbour)
        cubes = smooth_step(cubes, residual_of(cubes, rights, ghosts, wave_sq), wave_sq)
    ghosts = ghost_layers(cubes, neighbour)
    coarse_rows = restrict(residual_of(cubes, rights, ghosts, wave_sq))
    id_values = patch_of_slot.astype(jnp.float32)
    rows_all, wave_all, ids_all = (
        lax.all_gather(coarse_rows, "sub", axis=0, tiled=True),
        lax.all_gather(wave_sq, "sub", axis=0, tiled=True),
        lax.all_gather(id_values, "sub", axis=0, tiled=True),
    )
    selector = (ids_all[None, :] == jnp.arange(patch_total, dtype=jnp.float32)[:, None]).astype(
        jnp.float32
    )
    placed = jnp.dot(selector, rows_all, precision=lax.Precision.HIGHEST)
    placed_wave = jnp.dot(selector, wave_all[:, None], precision=lax.Precision.HIGHEST)[:, 0]
    coarse_rhs = (
        placed.reshape(rows_y, PZ, 2, small, small, small)
        .transpose(2, 3, 0, 4, 1, 5)
        .reshape(2, small, rows_y * small, PZ * small)
    )
    wave_grid = jnp.repeat(jnp.repeat(placed_wave.reshape(rows_y, PZ), small, 0), small, 1)
    coarse_wave = jnp.broadcast_to(wave_grid[None], (small,) + wave_grid.shape)
    correction = omega_coarse * coarse_divide(coarse_rhs, coarse_wave)
    for sweep_index in range(CITER - 1):
        padded = padded_2(correction, (("grp", 1),), 1)
        correction = correction + omega_coarse * coarse_divide(
            coarse_residual(padded, coarse_rhs, coarse_wave), coarse_wave
        )
    patch_blocks = (
        correction.reshape(2, small, rows_y, small, PZ, small)
        .transpose(2, 4, 0, 1, 3, 5)
        .reshape(patch_total, 2, small, small, small)
    )
    mine = patch_blocks[jnp.maximum(patch_of_slot, 0)]
    grown = jnp.broadcast_to(
        mine[:, :, :, None, :, None, :, None], (slot_count, 2, small, 4, small, 4, small, 4)
    ).reshape(slot_count, 2, edge, edge, edge)
    result = jnp.where((patch_of_slot >= 0)[:, None, None, None, None], cubes + grown, 0.0)
    return result.reshape(slot_count, 2, edge, edge * edge)


def solution(mesh):
    return jax.shard_map(
        body,
        mesh=mesh,
        in_specs=(
            P(("grp", "sub"), None, None, None),
            P(("grp", "sub"), None, None, None),
            P(("grp", "sub")),
            P(("grp", "sub"), None),
            P(("grp", "sub")),
            P(),
        ),
        out_specs=P(("grp", "sub"), None, None, None),
        check_vma=False,
    )
```

profile of v0, /device:TPU:0, one launch (start us, length us, event | category | flops | bytes accessed | tf_op | source)
XLA Modules:
  0.0 173.4 jit_solution(11633209185887477696)
XLA Ops:
  0.0 1.2 reshape.118
  2.9 6.9 %all_gather.18 = f32[16,6,2,256]{3,2,0,1:T(2,128)S(1)} all-gather(f32[4,6,2,256]{3,2,0,1:T(2,128)S(1)} %constant_dynamic-update-slice_fusion), channel_id=1, replica_groups=mesh['grp'=8,'sub'=4] {'sub'}, dimensions={0}, use_global_device_ids=true | all-gather | bytes 245760 | tf_op jit(solution)/shard_map/all_gather | solution.py:116
  10.4 4.2 %collective-permute-start = (f32[1,16,2,256]{3,2,1,0:T(2,128)S(1)}, f32[1,16,2,256]{3,2,1,0:T(2,128)}, u32[]{:S(2)}, u32[]{:S(2)}) collective-permute-start(f32[1,16,2,256]{3,2,1,0:T(2,128)S(1)} %get-tuple-element.130), channel_id=1, source_target_pairs={{0,4},{4,8},{8,12},{12,16},{16,20},{20,24},{24,28},{1,5},{5,9},{9,... | collective-permute-start | bytes 98312 | tf_op jit(solution)/shard_map/ppermute | solution.py:23
  14.6 1.3 collective-permute-start.1
  17.3 1.7 fusion.96
  19.0 1.6 fusion.97
  20.6 1.6 fusion.95
  26.4 6.9 %all-reduce.6 = (f32[16]{0:T(128)S(1)}, f32[16]{0:T(128)S(1)}) all-reduce(f32[16]{0:T(128)S(1)} %convert_dynamic-update-slice_fusion, f32[16]{0:T(128)S(1)} %dynamic-update-slice.5), channel_id=1, replica_groups=mesh['grp'=8,'sub'=4] {'sub'}, use_global_device_ids=true, to_apply=%add.4 | all-reduce | flops 32 | bytes 256
  35.5 1.5 copy.477
  41.7 1.1 copy.392
  42.8 2.0 %copy.394 = f32[4,2,16,1,16]{3,2,0,4,1:T(8,128)} copy(f32[4,2,16,1,16]{4,2,0,1,3:T(8,128)S(1)} %get-tuple-element.119) | data formatting | bytes 16384 | tf_op jit(solution)/shard_map/broadcast_in_dim;squeeze | solution.py:53
  45.0 4.0 %fusion.3 = f32[4,2,16,16,16]{3,2,0,4,1:T(8,128)S(1)} fusion(f32[4,2,15,16,16]{3,2,0,4,1:T(8,128)} %get-tuple-element.98, f32[4,2,1,16,16]{3,2,0,4,1:T(1,128)S(1)} %copy.388, f32[4,2,1,16,16]{3,2,0,4,1:T(1,128)S(1)} %copy.390, f32[4,2,15,16,16]{3,2,0,4,1:T(8,128)} %get-tuple-element.97, f32[4,2,16,15,16]{3,2,0,4,1:T(8,128)} %get-tuple-element.96, ...), kind=kLoop, calls=%fused_computation.11 | loop fusion | flops 360448 | bytes 917504 | tf_op jit(solution)/shard_map/add | solution.py:55
  50.7 1.7 fusion.93
  52.5 1.7 fusion.90
  54.2 1.6 fusion.91
  56.2 2.1 %copy.407 = f32[4,2,16,1,16]{4,2,1,0,3:T(8,128)S(1)} copy(f32[4,2,16,1,16]{3,2,0,4,1:T(8,128)} %get-tuple-element.90) | data formatting | bytes 16384 | tf_op jit(solution)/shard_map/slice | solution.py:38
  58.3 2.1 %copy.408 = f32[4,2,16,1,16]{4,2,1,0,3:T(8,128)S(1)} copy(f32[4,2,16,1,16]{3,2,0,4,1:T(8,128)} %get-tuple-element.89) | data formatting | bytes 16384 | tf_op jit(solution)/shard_map/slice | solution.py:39
  60.8 5.6 %all_gather.19 = f32[16,6,2,256]{3,2,1,0:T(2,128)S(1)} all-gather(f32[4,6,2,256]{3,2,1,0:T(2,128)S(1)} %copy.411), channel_id=1, replica_groups=mesh['grp'=8,'sub'=4] {'sub'}, dimensions={0}, use_global_device_ids=true | all-gather | bytes 245760 | tf_op jit(solution)/shard_map/all_gather | solution.py:116
  66.4 4.5 %collective-permute-start.2 = (f32[1,16,2,256]{3,2,1,0:T(2,128)S(1)}, f32[1,16,2,256]{3,2,1,0:T(2,128)S(1)}, u32[]{:S(2)}, u32[]{:S(2)}) collective-permute-start(f32[1,16,2,256]{3,2,1,0:T(2,128)S(1)} %get-tuple-element.128), channel_id=1, source_target_pairs={{0,4},{4,8},{8,12},{12,16},{16,20},{20,24},{24,28},{1,5},{5,9},{9,... | collective-permute-start | bytes 98312 | tf_op jit(solution)/shard_map/ppermute | solution.py:23
  70.9 1.6 fusion.89
  72.5 1.5 collective-permute-start.3
  74.0 4.3 %collective-permute-done.3 = f32[1,16,2,256]{3,2,1,0:T(2,128)S(1)} collective-permute-done((f32[1,16,2,256]{3,2,1,0:T(2,128)S(1)}, f32[1,16,2,256]{3,2,1,0:T(2,128)S(1)}, u32[]{:S(2)}, u32[]{:S(2)}) %collective-permute-start.3) | collective-permute-done | bytes 32800 | tf_op jit(solution)/shard_map/ppermute | solution.py:25
  81.5 2.0 %copy.417 = f32[4,2,16,1,16]{3,2,0,4,1:T(8,128)} copy(f32[4,2,16,1,16]{4,2,0,1,3:T(8,128)S(1)} %get-tuple-element.114) | data formatting | bytes 16384 | tf_op jit(solution)/shard_map/broadcast_in_dim;squeeze | solution.py:52
  83.4 1.9 %copy.418 = f32[4,2,16,1,16]{3,2,0,4,1:T(8,128)} copy(f32[4,2,16,1,16]{4,2,0,1,3:T(8,128)S(1)} %get-tuple-element.113) | data formatting | bytes 16384 | tf_op jit(solution)/shard_map/broadcast_in_dim;squeeze | solution.py:53
  85.6 4.3 %fusion.8 = f32[4,2,16,16,16]{3,2,0,4,1:T(8,128)S(1)} fusion(f32[4,2,15,16,16]{3,2,0,4,1:T(8,128)} %get-tuple-element.86, f32[4,2,1,16,16]{3,2,0,4,1:T(1,128)S(1)} %copy.415, f32[4,2,1,16,16]{3,2,0,4,1:T(1,128)S(1)} %copy.416, f32[4,2,15,16,16]{3,2,0,4,1:T(8,128)} %get-tuple-element.85, f32[4,2,16,15,16]{3,2,0,4,1:T(8,128)} %get-tuple-element.84, ...), kind=kLoop, calls=%fused_computation.18 | loop fusion | flops 360448 | bytes 917504 | tf_op jit(solution)/shard_map/add | solution.py:55
  91.4 1.4 fusion.87
  92.9 1.7 %fusion.84 = (f32[4,2,16,15,16]{3,2,1,0,4:T(8,128)}, f32[4,2,16,15,16]{3,2,1,0,4:T(8,128)}) fusion(f32[4,2,16,16,16]{3,2,1,0,4:T(8,128)S(1)} %copy_add_fusion), kind=kLoop, calls=%fused_computation.211 | loop fusion | bytes 491520 | tf_op jit(solution)/shard_map/slice | solution.py:53
  94.6 1.6 fusion.85
  96.3 2.1 %copy.431 = f32[4,2,16,1,16]{4,2,1,0,3:T(8,128)S(1)} copy(f32[4,2,16,1,16]{3,2,1,0,4:T(8,128)} %get-tuple-element.78) | data formatting | bytes 16384 | tf_op jit(solution)/shard_map/slice | solution.py:38
  100.0 5.6 %all_gather.21 = f32[16,6,2,256]{3,2,1,0:T(2,128)S(1)} all-gather(f32[4,6,2,256]{3,2,1,0:T(2,128)S(1)} %copy.433), channel_id=1, replica_groups=mesh['grp'=8,'sub'=4] {'sub'}, dimensions={0}, use_global_device_ids=true | all-gather | bytes 245760 | tf_op jit(solution)/shard_map/all_gather | solution.py:116
  105.7 4.7 %collective-permute-start.4 = (f32[1,16,2,256]{3,2,1,0:T(2,128)S(1)}, f32[1,16,2,256]{3,2,1,0:T(2,128)S(1)}, u32[]{:S(2)}, u32[]{:S(2)}) collective-permute-start(f32[1,16,2,256]{3,2,1,0:T(2,128)S(1)} %get-tuple-element.126), channel_id=1, source_target_pairs={{0,4},{4,8},{8,12},{12,16},{16,20},{20,24},{24,28},{1,5},{5,9},{9,... | collective-permute-start | bytes 98312 | tf_op jit(solution)/shard_map/ppermute | solution.py:23
  110.4 1.6 fusion.83
  111.9 1.5 collective-permute-start.5
  113.5 4.3 %collective-permute-done.5 = f32[1,16,2,256]{3,2,1,0:T(2,128)S(1)} collective-permute-done((f32[1,16,2,256]{3,2,1,0:T(2,128)S(1)}, f32[1,16,2,256]{3,2,1,0:T(2,128)S(1)}, u32[]{:S(2)}, u32[]{:S(2)}) %collective-permute-start.5) | collective-permute-done | bytes 32800 | tf_op jit(solution)/shard_map/ppermute | solution.py:25
  120.0 2.0 %copy.444 = f32[4,2,16,1,16]{3,2,0,4,1:T(8,128)} copy(f32[4,2,16,1,16]{4,2,0,1,3:T(8,128)S(1)} %get-tuple-element.107) | data formatting | bytes 16384 | tf_op jit(solution)/shard_map/broadcast_in_dim;squeeze | solution.py:53
  122.1 3.9 %fusion.12 = f32[4,2,16,16,16]{3,2,0,4,1:T(8,128)S(1)} fusion(f32[4,2,1,16,16]{3,2,0,4,1:T(1,128)S(1)} %copy.438, f32[4,2,1,16,16]{3,2,0,4,1:T(1,128)S(1)} %copy.440, f32[4,2,16,1,16]{3,2,0,4,1:T(8,128)S(1)} %copy.442, f32[4,2,16,1,16]{3,2,0,4,1:T(8,128)} %copy.444, f32[4,2,16,16,1]{3,2,0,4,1:T(8,128)S(1)} %get-tuple-element.106, ...), kind=kLoop, calls=%fused_computation.24 | loop fusion | flops 360448 | bytes 917504 | tf_op jit(solution)/shard_map/add | solution.py:55
  127.2 2.1 %stack.124 = f32[4,1,4,4,4,4,4,4]{5,4,3,2,0,7,6,1:T(4,128)S(1)} reshape(f32[4,1,16,16,16]{3,2,0,4,1:T(8,128)} %fusion.17) | data formatting | bytes 131072 | tf_op jit(solution)/shard_map/stack | solution.py:66
  129.4 2.3 %stack.125 = f32[4,1,4,4,4,4,4,4]{5,4,3,2,0,7,6,1:T(4,128)} reshape(f32[4,1,16,16,16]{3,2,1,0,4:T(8,128)S(1)} %fusion.15) | data formatting | bytes 131072 | tf_op jit(solution)/shard_map/stack | solution.py:66
  131.6 3.1 %maximum_reduce_fusion = f32[4,2,4,4,4]{3,2,0,4,1:T(4,128)S(1)} fusion(f32[4,1,4,4,4,4,4,4]{5,4,3,2,0,7,6,1:T(4,128)} %stack.125, f32[4,1,4,4,4,4,4,4]{5,4,3,2,0,7,6,1:T(4,128)S(1)} %stack.124), kind=kLoop, calls=%fused_computation.4 | loop fusion | flops 65024 | bytes 133120 | tf_op jit(solution)/shard_map/reduce_sum | solution.py:89
  135.2 5.2 %all-gather = f32[4,4,128]{2,1,0:T(4,128)S(1)} all-gather(f32[1,4,128]{2,1,0:T(4,128)S(1)} %reshape.287), channel_id=1, replica_groups=mesh['grp'=8,'sub'=4] {'sub'}, dimensions={0}, use_global_device_ids=true | all-gather | bytes 10240 | tf_op jit(solution)/shard_map/all_gather | solution.py:147
  141.2 2.9 %collective-permute-start.6 = (f32[2,1,12,16]{3,1,2,0:T(1,128)S(1)}, f32[2,1,12,16]{3,1,2,0:T(1,128)S(1)}, u32[]{:S(2)}, u32[]{:S(2)}) collective-permute-start(f32[2,1,12,16]{3,1,2,0:T(1,128)S(1)} %get-tuple-element.135), channel_id=1, source_target_pairs={{0,4},{4,8},{8,12},{12,16},{16,20},{20,24},{24,28},{1,5},{5,9},{9,... | collective-permute-start | bytes 4616 | tf_op jit(solution)/shard_map/ppermute | solution.py:23
  144.2 1.3 collective-permute-start.7
  145.7 4.0 %collective-permute-done.7 = f32[2,1,12,16]{3,1,2,0:T(1,128)S(1)} collective-permute-done((f32[2,1,12,16]{3,1,2,0:T(1,128)S(1)}, f32[2,1,12,16]{3,1,2,0:T(1,128)S(1)}, u32[]{:S(2)}, u32[]{:S(2)}) %collective-permute-start.7) | collective-permute-done | bytes 1568 | tf_op jit(solution)/shard_map/ppermute | solution.py:25
  150.7 5.4 %collective-permute-start.8 = (f32[2,1,12,16]{3,1,2,0:T(1,128)}, f32[2,1,12,16]{3,1,2,0:T(1,128)}, u32[]{:S(2)}, u32[]{:S(2)}) collective-permute-start(f32[2,1,12,16]{3,1,2,0:T(1,128)} %get-tuple-element.133), channel_id=1, source_target_pairs={{0,4},{4,8},{8,12},{12,16},{16,20},{20,24},{24,28},{1,5},{5,9},{9,... | collective-permute-start | bytes 4616 | tf_op jit(solution)/shard_map/ppermute | solution.py:23
  156.1 1.5 collective-permute-start.9
  160.4 1.3 collective-permute-done.9
  163.8 2.6 %broadcast_in_dim.119 = f32[4,2,4,4,4,4,4,4]{7,6,5,4,3,2,1,0:T(4,128)} broadcast(f32[4,2,4,4,4]{4,3,2,1,0:T(4,128)S(1)} %gather_fusion.3), dimensions={0,1,2,4,6} | broadcast | bytes 133120 | tf_op jit(solution)/shard_map/broadcast_in_dim | solution.py:175
  166.4 6.3 %reshape.123 = f32[4,2,16,256]{3,2,1,0:T(8,128)S(1)} reshape(f32[4,2,4,4,4,4,4,4]{7,6,5,4,3,2,1,0:T(4,128)} %broadcast_in_dim.119) | data formatting | bytes 262144 | tf_op jit(solution)/shard_map/reshape | solution.py:177
  (254 shorter events, 34.5 us)
Async XLA Ops:
  0.0 15.9 %copy-start.30 = (s32[4,6]{1,0:T(4,128)S(1)}, s32[4,6]{1,0:T(4,128)}, u32[]{:S(2)}) copy-start(s32[4,6]{1,0:T(4,128)} %param.17) | copy-start | bytes 292
  10.4 28.1 %collective-permute-start = (f32[1,16,2,256]{3,2,1,0:T(2,128)S(1)}, f32[1,16,2,256]{3,2,1,0:T(2,128)}, u32[]{:S(2)}, u32[]{:S(2)}) collective-permute-start(f32[1,16,2,256]{3,2,1,0:T(2,128)S(1)} %get-tuple-element.130), channel_id=1, source_target_pairs={{0,4},{4,8},{8,12},{12,16},{16,20},{20,24},{24,28},{1,5},{5,9},{9,... | collective-permute-start | bytes 98312 | tf_op jit(solution)/shard_map/ppermute | solution.py:23
  14.6 24.7 %collective-permute-start.1 = (f32[1,16,2,256]{3,2,1,0:T(2,128)}, f32[1,16,2,256]{3,2,1,0:T(2,128)}, u32[]{:S(2)}, u32[]{:S(2)}) collective-permute-start(f32[1,16,2,256]{3,2,1,0:T(2,128)} %get-tuple-element.129), channel_id=1, source_target_pairs={{4,0},{8,4},{12,8},{16,12},{20,16},{24,20},{28,24},{5,1},{9,5},{13... | collective-permute-start | bytes 98312 | tf_op jit(solution)/shard_map/ppermute | solution.py:25
  19.0 3.2 %copy-start.36 = (f32[16]{0:T(128)S(1)}, f32[16]{0:T(128)}, u32[]{:S(2)}) copy-start(f32[16]{0:T(128)} %param.19) | copy-start | bytes 196
  19.0 3.2 %copy-start.37 = (s32[4]{0:T(128)S(1)}, s32[4]{0:T(128)}, u32[]{:S(2)}) copy-start(s32[4]{0:T(128)} %param.18) | copy-start | bytes 52
  19.0 4.0 %copy-start.21 = (f32[4,2,16,256]{3,2,1,0:T(8,128)S(1)}, f32[4,2,16,256]{3,2,1,0:T(8,128)}, u32[]{:S(2)}) copy-start(f32[4,2,16,256]{3,2,1,0:T(8,128)} %param.15) | copy-start | bytes 393220
  20.6 3.6 %copy-start.38 = (s32[4]{0:T(128)S(1)}, s32[4]{0:T(128)}, u32[]{:S(2)}) copy-start(s32[4]{0:T(128)} %param.16) | copy-start | bytes 52
  20.6 4.2 %copy-start.39 = (u32[32]{0:T(128)S(1)}, u32[32]{0:T(128)}, u32[]{:S(2)}) copy-start(u32[32]{0:T(128)} %constant.256) | copy-start | bytes 388
  22.4 11.9 %copy-start.27 = (f32[4]{0:T(128)}, f32[4]{0:T(128)S(1)}, u32[]{:S(2)}) copy-start(f32[4]{0:T(128)S(1)} %select_reduce_fusion) | copy-start | bytes 52
  44.9 4.0 %copy-start.23 = (f32[4]{0:T(128)S(1)}, f32[4]{0:T(128)}, u32[]{:S(2)}) copy-start(f32[4]{0:T(128)} %get-tuple-element.141) | copy-start | bytes 52
  45.0 4.0 %copy-start.25 = (f32[4]{0:T(128)S(1)}, f32[4]{0:T(128)}, u32[]{:S(2)}) copy-start(f32[4]{0:T(128)} %get-tuple-element.142) | copy-start | bytes 52
  45.0 4.0 %copy-start.28 = (f32[4]{0:T(128)S(1)}, f32[4]{0:T(128)}, u32[]{:S(2)}) copy-start(f32[4]{0:T(128)} %copy-done.27) | copy-start | bytes 52
  49.4 3.0 %copy-start = (f32[4,16,16,16]{2,1,0,3:T(8,128)}, f32[4,16,16,16]{2,1,0,3:T(8,128)S(1)}, u32[]{:S(2)}) copy-start(f32[4,16,16,16]{2,1,0,3:T(8,128)S(1)} %get-tuple-element.66) | copy-start | bytes 196612
  66.4 7.6 %collective-permute-start.2 = (f32[1,16,2,256]{3,2,1,0:T(2,128)S(1)}, f32[1,16,2,256]{3,2,1,0:T(2,128)S(1)}, u32[]{:S(2)}, u32[]{:S(2)}) collective-permute-start(f32[1,16,2,256]{3,2,1,0:T(2,128)S(1)} %get-tuple-element.128), channel_id=1, source_target_pairs={{0,4},{4,8},{8,12},{12,16},{16,20},{20,24},{24,28},{1,5},{5,9},{9,... | collective-permute-start | bytes 98312 | tf_op jit(solution)/shard_map/ppermute | solution.py:23
  72.5 5.8 %collective-permute-start.3 = (f32[1,16,2,256]{3,2,1,0:T(2,128)S(1)}, f32[1,16,2,256]{3,2,1,0:T(2,128)S(1)}, u32[]{:S(2)}, u32[]{:S(2)}) collective-permute-start(f32[1,16,2,256]{3,2,1,0:T(2,128)S(1)} %get-tuple-element.127), channel_id=1, source_target_pairs={{4,0},{8,4},{12,8},{16,12},{20,16},{24,20},{28,24},{5,1},{9,5},{13... | collective-permute-start | bytes 98312 | tf_op jit(solution)/shard_map/ppermute | solution.py:25
  85.5 4.3 %copy-start.24 = (f32[4]{0:T(128)S(1)}, f32[4]{0:T(128)}, u32[]{:S(2)}) copy-start(f32[4]{0:T(128)} %get-tuple-element.141) | copy-start | bytes 52
  85.5 4.3 %copy-start.26 = (f32[4]{0:T(128)S(1)}, f32[4]{0:T(128)}, u32[]{:S(2)}) copy-start(f32[4]{0:T(128)} %get-tuple-element.142) | copy-start | bytes 52
  85.6 4.3 %copy-start.29 = (f32[4]{0:T(128)S(1)}, f32[4]{0:T(128)}, u32[]{:S(2)}) copy-start(f32[4]{0:T(128)} %copy-done.27) | copy-start | bytes 52
  89.9 1.0 copy-start.1
  89.9 1.2 copy-start.4
  90.3 2.4 %copy-start.6 = (f32[4,16,16,16]{2,1,0,3:T(8,128)}, f32[4,16,16,16]{2,1,0,3:T(8,128)S(1)}, u32[]{:S(2)}) copy-start(f32[4,16,16,16]{2,1,0,3:T(8,128)S(1)} %get-tuple-element.63) | copy-start | bytes 196612
  90.5 2.3 %copy-start.8 = (f32[4,16,16,16]{2,1,0,3:T(8,128)}, f32[4,16,16,16]{2,1,0,3:T(8,128)S(1)}, u32[]{:S(2)}) copy-start(f32[4,16,16,16]{2,1,0,3:T(8,128)S(1)} %add_divide_fusion) | copy-start | bytes 196612
  96.3 22.5 %copy-start.31 = (pred[4,6]{1,0:T(4,128)(4,1)S(1)}, pred[4,6]{1,0:T(4,128)(4,1)}, u32[]{:S(2)}) copy-start(pred[4,6]{1,0:T(4,128)(4,1)} %broadcast_compare_fusion) | copy-start | bytes 76
  105.7 7.8 %collective-permute-start.4 = (f32[1,16,2,256]{3,2,1,0:T(2,128)S(1)}, f32[1,16,2,256]{3,2,1,0:T(2,128)S(1)}, u32[]{:S(2)}, u32[]{:S(2)}) collective-permute-start(f32[1,16,2,256]{3,2,1,0:T(2,128)S(1)} %get-tuple-element.126), channel_id=1, source_target_pairs={{0,4},{4,8},{8,12},{12,16},{16,20},{20,24},{24,28},{1,5},{5,9},{9,... | collective-permute-start | bytes 98312 | tf_op jit(solution)/shard_map/ppermute | solution.py:23
  111.9 5.8 %collective-permute-start.5 = (f32[1,16,2,256]{3,2,1,0:T(2,128)S(1)}, f32[1,16,2,256]{3,2,1,0:T(2,128)S(1)}, u32[]{:S(2)}, u32[]{:S(2)}) collective-permute-start(f32[1,16,2,256]{3,2,1,0:T(2,128)S(1)} %get-tuple-element.125), channel_id=1, source_target_pairs={{4,0},{8,4},{12,8},{16,12},{20,16},{24,20},{28,24},{5,1},{9,5},{13... | collective-permute-start | bytes 98312 | tf_op jit(solution)/shard_map/ppermute | solution.py:25
  129.3 11.1 %copy-start.34 = (f32[16]{0:T(128)S(1)}, f32[16]{0:T(128)}, u32[]{:S(2)}) copy-start(f32[16]{0:T(128)} %copy-done.33) | copy-start | bytes 196
  129.3 11.8 %copy-start.11 = (f32[12,16]{1,0:T(8,128)S(1)}, f32[12,16]{1,0:T(8,128)}, u32[]{:S(2)}) copy-start(f32[12,16]{1,0:T(8,128)} %copy.458) | copy-start | bytes 2308
  129.3 11.8 %copy-start.12 = (f32[12,16]{1,0:T(8,128)S(1)}, f32[12,16]{1,0:T(8,128)}, u32[]{:S(2)}) copy-start(f32[12,16]{1,0:T(8,128)} %copy.459) | copy-start | bytes 2308
  129.4 20.5 %copy-start.22 = (f32[12,16]{1,0:T(8,128)S(1)}, f32[12,16]{1,0:T(8,128)}, u32[]{:S(2)}) copy-start(f32[12,16]{1,0:T(8,128)} %copy.460) | copy-start | bytes 2308
  129.4 28.3 %copy-start.32 = (s32[4]{0:T(128)S(1)}, s32[4]{0:T(128)}, u32[]{:S(2)}) copy-start(s32[4]{0:T(128)} %broadcast_maximum_fusion) | copy-start | bytes 52
  131.6 26.0 %copy-start.5 = (f32[4,16,16,16]{2,1,0,3:T(8,128)S(1)}, f32[4,16,16,16]{2,1,0,3:T(8,128)}, u32[]{:S(2)}) copy-start(f32[4,16,16,16]{2,1,0,3:T(8,128)} %copy-done.3) | copy-start | bytes 196612
  131.6 26.4 %copy-start.2 = (f32[4,16,16,16]{2,1,0,3:T(8,128)S(1)}, f32[4,16,16,16]{2,1,0,3:T(8,128)}, u32[]{:S(2)}) copy-start(f32[4,16,16,16]{2,1,0,3:T(8,128)} %copy-done) | copy-start | bytes 196612
  134.8 24.1 %copy-start.9 = (f32[4,16,16,16]{2,1,0,3:T(8,128)S(1)}, f32[4,16,16,16]{2,1,0,3:T(8,128)}, u32[]{:S(2)}) copy-start(f32[4,16,16,16]{2,1,0,3:T(8,128)} %copy-done.8) | copy-start | bytes 196612
  134.8 24.3 %copy-start.7 = (f32[4,16,16,16]{2,1,0,3:T(8,128)S(1)}, f32[4,16,16,16]{2,1,0,3:T(8,128)}, u32[]{:S(2)}) copy-start(f32[4,16,16,16]{2,1,0,3:T(8,128)} %copy-done.6) | copy-start | bytes 196612
  141.2 4.5 %collective-permute-start.6 = (f32[2,1,12,16]{3,1,2,0:T(1,128)S(1)}, f32[2,1,12,16]{3,1,2,0:T(1,128)S(1)}, u32[]{:S(2)}, u32[]{:S(2)}) collective-permute-start(f32[2,1,12,16]{3,1,2,0:T(1,128)S(1)} %get-tuple-element.135), channel_id=1, source_target_pairs={{0,4},{4,8},{8,12},{12,16},{16,20},{20,24},{24,28},{1,5},{5,9},{9,... | collective-permute-start | bytes 4616 | tf_op jit(solution)/shard_map/ppermute | solution.py:23
  144.2 5.6 %collective-permute-start.7 = (f32[2,1,12,16]{3,1,2,0:T(1,128)S(1)}, f32[2,1,12,16]{3,1,2,0:T(1,128)S(1)}, u32[]{:S(2)}, u32[]{:S(2)}) collective-permute-start(f32[2,1,12,16]{3,1,2,0:T(1,128)S(1)} %get-tuple-element.136), channel_id=1, source_target_pairs={{4,0},{8,4},{12,8},{16,12},{20,16},{24,20},{28,24},{5,1},{9,5},{13... | collective-permute-start | bytes 4616 | tf_op jit(solution)/shard_map/ppermute | solution.py:25
  145.6 4.4 %copy-start.17 = (f32[1,4,12,16]{3,1,2,0:T(4,128)}, f32[1,4,12,16]{3,1,2,0:T(4,128)S(1)}, u32[]{:S(2)}) copy-start(f32[1,4,12,16]{3,1,2,0:T(4,128)S(1)} %squeeze.4) | copy-start | bytes 9220
  145.7 4.3 %copy-start.19 = (f32[1,4,12,16]{3,1,2,0:T(4,128)}, f32[1,4,12,16]{3,1,2,0:T(4,128)S(1)}, u32[]{:S(2)}) copy-start(f32[1,4,12,16]{3,1,2,0:T(4,128)S(1)} %squeeze.5) | copy-start | bytes 9220
  149.9 7.7 %copy-start.15 = (f32[4,12,16]{2,0,1:T(4,128)}, f32[4,12,16]{2,0,1:T(4,128)S(1)}, u32[]{:S(2)}) copy-start(f32[4,12,16]{2,0,1:T(4,128)S(1)} %get-tuple-element.60) | copy-start | bytes 9220
  150.0 8.0 %copy-start.13 = (f32[4,12,16]{2,0,1:T(4,128)}, f32[4,12,16]{2,0,1:T(4,128)S(1)}, u32[]{:S(2)}) copy-start(f32[4,12,16]{2,0,1:T(4,128)S(1)} %add_divide_fusion.3) | copy-start | bytes 9220
  150.7 9.7 %collective-permute-start.8 = (f32[2,1,12,16]{3,1,2,0:T(1,128)}, f32[2,1,12,16]{3,1,2,0:T(1,128)}, u32[]{:S(2)}, u32[]{:S(2)}) collective-permute-start(f32[2,1,12,16]{3,1,2,0:T(1,128)} %get-tuple-element.133), channel_id=1, source_target_pairs={{0,4},{4,8},{8,12},{12,16},{16,20},{20,24},{24,28},{1,5},{5,9},{9,... | collective-permute-start | bytes 4616 | tf_op jit(solution)/shard_map/ppermute | solution.py:23
  156.1 5.7 %collective-permute-start.9 = (f32[2,1,12,16]{3,1,2,0:T(1,128)S(1)}, f32[2,1,12,16]{3,1,2,0:T(1,128)}, u32[]{:S(2)}, u32[]{:S(2)}) collective-permute-start(f32[2,1,12,16]{3,1,2,0:T(1,128)S(1)} %get-tuple-element.134), channel_id=1, source_target_pairs={{4,0},{8,4},{12,8},{16,12},{20,16},{24,20},{28,24},{5,1},{9,5},{13... | collective-permute-start | bytes 4616 | tf_op jit(solution)/shard_map/ppermute | solution.py:25
  158.0 2.3 %copy-start.16 = (f32[4,12,16]{2,0,1:T(4,128)S(1)}, f32[4,12,16]{2,0,1:T(4,128)}, u32[]{:S(2)}) copy-start(f32[4,12,16]{2,0,1:T(4,128)} %copy-done.15) | copy-start | bytes 9220
  158.0 4.6 %copy-start.18 = (f32[1,4,12,16]{3,1,2,0:T(4,128)S(1)}, f32[1,4,12,16]{3,1,2,0:T(4,128)}, u32[]{:S(2)}) copy-start(f32[1,4,12,16]{3,1,2,0:T(4,128)} %copy-done.17) | copy-start | bytes 9220
  158.0 4.6 %copy-start.20 = (f32[1,4,12,16]{3,1,2,0:T(4,128)S(1)}, f32[1,4,12,16]{3,1,2,0:T(4,128)}, u32[]{:S(2)}) copy-start(f32[1,4,12,16]{3,1,2,0:T(4,128)} %copy-done.19) | copy-start | bytes 9220
  158.3 1.8 %copy-start.14 = (f32[4,12,16]{2,0,1:T(4,128)S(1)}, f32[4,12,16]{2,0,1:T(4,128)}, u32[]{:S(2)}) copy-start(f32[4,12,16]{2,0,1:T(4,128)} %copy-done.13) | copy-start | bytes 9220
  163.8 8.9 %copy-start.10 = (f32[4,2,16,256]{3,2,1,0:T(8,128)S(1)}, f32[4,2,16,256]{3,2,1,0:T(8,128)}, u32[]{:S(2)}) copy-start(f32[4,2,16,256]{3,2,1,0:T(8,128)} %param.14) | copy-start | bytes 393220
  163.8 8.9 %copy-start.35 = (pred[4]{0:T(512)(128)(4,1)S(1)}, pred[4]{0:T(512)(128)(4,1)}, u32[]{:S(2)}) copy-start(pred[4]{0:T(512)(128)(4,1)} %broadcast_compare_fusion.1) | copy-start | bytes 16
  (2 other events, 1.3 us)
where the time goes:
time: 174 us; the launch traced here: 173 us
  local copies, waits for them, and re-layouts  74.1 us (43%)
  blocking collectives  30.1 us (17%)
  starting transfers between devices  28.8 us (17%)
  other arithmetic  24.2 us (14%)
  waiting for transfers between devices  13.9 us (8%)
  between operations  1.96 us (1%)
    ppermute x5, starting transfers between devices, padded_2(): lax.ppermute(tail, axis, [(i, (i + 1) % count) for i in range(ends)])  21.7 us
    all_gather x3, blocking collectives, ghost_layers(): table = lax.all_gather(own_faces, 'sub', axis=0, tiled=True)  18.1 us
    ppermute x5, waiting for transfers between devices, padded_2(): lax.ppermute(head, axis, [((i + 1) % count, i) for i in range(ends)])  13.9 us
    add x3, other arithmetic, neighbour_sum(): total + jnp.concatenate([cubes[..., 1:], ghost_sheets[:, 5][..., None]], 4)  12.2 us
    ppermute x5, starting transfers between devices, padded_2(): lax.ppermute(head, axis, [((i + 1) % count, i) for i in range(ends)])  7.07 us
    unnamed x1, blocking collectives  6.86 us
    unnamed x118, local copies, waits for them, and re-layouts  6.32 us
    reshape x1, local copies, waits for them, and re-layouts, body(): grown = jnp.broadcast_to(mine[:, :, :, None, :, None, :, None], (slot_cou...  6.28 us
  transfers between devices with their start and end apart: 10, of which 4 were waited for; matrix products, arithmetic and copies ran while one was open for 13% of the time, Pallas kernels for 0%

commit v1 on v0

v1 whole, which is shorter than its diff:
```python
import functools

import jax
import jax.numpy as jnp
from jax import lax
from jax.experimental import pallas as pl
from jax.experimental.pallas import tpu as pltpu
from jax.sharding import PartitionSpec as P

PZ = 4
CITER = 3
ROUNDS = 3

omega_fine = 0.7
omega_coarse = 0.6
shift_imag = 0.5

F32 = jnp.float32
BF16 = jnp.bfloat16
MESH = pl.DeviceIdType.MESH


def iota(shape, axis):
    return lax.broadcasted_iota(jnp.int32, shape, axis)


def terms_of(values, count):
    terms = []
    for _ in range(count - 1):
        term = values.astype(BF16)
        terms.append(term)
        values = values - term.astype(F32)
    terms.append(values.astype(BF16))
    return terms


def times_selector(values, selector, count=2):
    rows = values.shape[0]
    stacked = jnp.concatenate(terms_of(values, count), 0)
    product = jnp.dot(stacked, selector, preferred_element_type=F32)
    total = product[:rows]
    for term in range(1, count):
        total = total + product[term * rows : (term + 1) * rows]
    return total


def face_cells(shape, lane_axis, opposite):
    lane = iota(shape, lane_axis)
    face = lane >> 5
    if opposite:
        face = face ^ 1
    place = lane & 15
    cell = jnp.where(
        face < 2,
        place + jnp.where(face == 1, 240, 0),
        place * 16 + jnp.where(face == 3, 15, 0),
    )
    return (lane >> 4) & 1, cell


def pack_matrix():
    shape = (512, 128)
    part, cell = face_cells(shape, 1, False)
    return (iota(shape, 0) == part * 256 + cell).astype(F32).astype(BF16)


def unpack_matrix():
    shape = (128, 512)
    part, cell = face_cells(shape, 0, True)
    return (iota(shape, 1) == part * 256 + cell).astype(F32).astype(BF16)


def block_match(fine, lane):
    same_part = (fine >> 8) == (lane >> 6)
    same_y = ((fine >> 6) & 3) == ((lane >> 2) & 3)
    same_z = ((fine >> 2) & 3) == (lane & 3)
    return (same_part & same_y & same_z).astype(F32).astype(BF16)


def kernel(
    n_grp,
    n_sub,
    patch_ref,
    link_ref,
    index_ref,
    table_ref,
    field_ref,
    source_ref,
    out_ref,
    faces_0,
    faces_1,
    faces_2,
    below_0,
    below_1,
    below_2,
    above_0,
    above_1,
    above_2,
    sheets,
    meta,
    rows,
    placed_e,
    slab_send,
    slab_recv,
    low_send,
    low_recv,
    high_send,
    high_recv,
):
    faces = (faces_0, faces_1, faces_2)
    below = (below_0, below_1, below_2)
    above = (above_0, above_1, above_2)
    slots = field_ref.shape[0]
    fine_rows = slots * 16
    patch_total = 3 * n_sub
    rows_y = patch_total // PZ
    patch_rows = -(-patch_total // 8) * 8
    g = lax.axis_index("grp")
    s = lax.axis_index("sub")
    has_low = g > 0
    has_high = g < n_grp - 1

    def beside(step):
        return lax.rem(s + step, n_sub)

    def before(step):
        return lax.rem(s + n_sub - step, n_sub)

    barrier = pltpu.get_barrier_semaphore()
    for step in range(1, n_sub):
        pl.semaphore_signal(barrier, inc=1, device_id=(g, beside(step)), device_id_type=MESH)

    @pl.when(has_low)
    def _():
        for step in range(n_sub):
            pl.semaphore_signal(
                barrier, inc=1, device_id=(g - 1, beside(step)), device_id_type=MESH
            )

    @pl.when(has_high)
    def _():
        for step in range(n_sub):
            pl.semaphore_signal(
                barrier, inc=1, device_id=(g + 1, beside(step)), device_id_type=MESH
            )

    def slab_copy(ref_of, stage, step, owner):
        ref = ref_of(owner)
        return pltpu.make_async_remote_copy(
            src_ref=ref,
            dst_ref=ref,
            send_sem=slab_send.at[stage, step],
            recv_sem=slab_recv.at[stage, step],
            device_id=(g, beside(step)),
            device_id_type=MESH,
        )

    def low_copy(src, dst, stage, step):
        return pltpu.make_async_remote_copy(
            src_ref=src,
            dst_ref=dst,
            send_sem=low_send.at[stage, step],
            recv_sem=high_recv.at[stage, step],
            device_id=(g - 1, beside(step)),
            device_id_type=MESH,
        )

    def high_copy(src, dst, stage, step):
        return pltpu.make_async_remote_copy(
            src_ref=src,
            dst_ref=dst,
            send_sem=high_send.at[stage, step],
            recv_sem=low_recv.at[stage, step],
            device_id=(g + 1, beside(step)),
            device_id_type=MESH,
        )

    def send(stage, slab_of, low_src, low_of, high_src, high_of):
        @pl.when(has_high)
        def _():
            for step in range(n_sub):
                high_copy(high_src, low_of(s), stage, step).start()

        @pl.when(has_low)
        def _():
            for step in range(n_sub):
                low_copy(low_src, high_of(s), stage, step).start()

        for step in range(1, n_sub):
            slab_copy(slab_of, stage, step, s).start()

    def receive(stage, slab_of, low_src, low_of, high_src, high_of):
        for step in range(1, n_sub):
            slab_copy(slab_of, stage, step, before(step)).wait_recv()

        @pl.when(has_low)
        def _():
            for step in range(n_sub):
                high_copy(high_src, low_of(before(step)), stage, step).wait_recv()

        @pl.when(has_high)
        def _():
            for step in range(n_sub):
                low_copy(low_src, high_of(before(step)), stage, step).wait_recv()

    def sent(stage, slab_of, low_src, low_of, high_src, high_of):
        for step in range(1, n_sub):
            slab_copy(slab_of, stage, step, s).wait_send()

        @pl.when(has_high)
        def _():
            for step in range(n_sub):
                high_copy(high_src, low_of(s), stage, step).wait_send()

        @pl.when(has_low)
        def _():
            for step in range(n_sub):
                low_copy(low_src, high_of(s), stage, step).wait_send()

    def face_exchange(stage):
        return (
            stage,
            lambda owner: faces[stage].at[pl.ds(owner * slots, slots)],
            sheets.at[stage, 0],
            lambda owner: below[stage].at[owner],
            sheets.at[stage, 1],
            lambda owner: above[stage].at[owner],
        )

    def row_exchange(stage, ref):
        mine = ref.at[1, s]
        return (
            stage,
            lambda owner: ref.at[1, owner],
            mine,
            lambda owner: ref.at[0, owner],
            mine,
            lambda owner: ref.at[2, owner],
        )

    meta_exchange = row_exchange(ROUNDS, meta)
    coarse_exchange = row_exchange(ROUNDS + 1, rows)

    @pl.when(jnp.logical_not(has_low))
    def _():
        for layers in below:
            layers[...] = jnp.zeros_like(layers)
        meta[0] = jnp.zeros_like(meta[0])
        rows[0] = jnp.zeros_like(rows[0])

    @pl.when(jnp.logical_not(has_high))
    def _():
        for layers in above:
            layers[...] = jnp.zeros_like(layers)
        meta[2] = jnp.zeros_like(meta[2])
        rows[2] = jnp.zeros_like(rows[2])

    wave_of = [table_ref[index_ref[slot]] for slot in range(slots)]
    patch_of = [patch_ref[slot] for slot in range(slots)]

    row8 = iota((8, 128), 0)
    meta_rows = jnp.zeros((8, 128), F32)
    for slot in range(slots):
        meta_rows = jnp.where(row8 == slot, wave_of[slot], meta_rows)
        meta_rows = jnp.where(
            row8 == slots + slot, (patch_of[slot] + 1).astype(F32), meta_rows
        )
    meta[1, s] = meta_rows

    def joined(ref, part):
        return jnp.concatenate([ref[slot, part] for slot in range(slots)], 0)

    real = joined(field_ref, 0)
    imag = joined(field_ref, 1)

    pack = pack_matrix()

    def put_faces(stage, real, imag):
        packed = times_selector(jnp.concatenate([real, imag], 1), pack)
        for slot in range(slots):
            faces[stage][s * slots + slot] = packed[slot * 16 : slot * 16 + 16]
        for side, edge_row in ((0, 0), (1, 15)):
            lines = []
            for half in range(2):
                for slot in range(slots):
                    for values in (real, imag):
                        row = slot * 16 + edge_row
                        lines.append(values[row : row + 1, half * 128 : half * 128 + 128])
            sheets[stage, side] = jnp.concatenate(lines, 0)

    put_faces(0, real, imag)

    greeted = n_sub - 1 + n_sub * (has_low.astype(jnp.int32) + has_high.astype(jnp.int32))
    pl.semaphore_wait(barrier, greeted)

    send(*face_exchange(0))
    send(*meta_exchange)

    source_real = joined(source_ref, 0)
    source_imag = joined(source_ref, 1)
    unpack = unpack_matrix()
    wave = jnp.concatenate([jnp.full((16, 256), wave_of[slot], F32) for slot in range(slots)], 0)
    real_diag = 6.0 - wave
    imag_diag = shift_imag * wave
    scale = omega_fine / (real_diag * real_diag + imag_diag * imag_diag)
    step_real = real_diag * scale
    step_imag = imag_diag * scale

    cell = iota((fine_rows, 256), 1)
    fine_i = iota((fine_rows, 256), 0) & 15
    y_low = cell < 16
    y_high = cell >= 240
    z_low = (cell & 15) == 0
    z_high = (cell & 15) == 15
    x_low = fine_i == 0
    x_high = fine_i == 15

    def inner_sum(values):
        total = jnp.where(y_low, 0.0, pltpu.roll(values, 16, 1))
        total = total + jnp.where(y_high, 0.0, pltpu.roll(values, 240, 1))
        total = total + jnp.where(z_low, 0.0, pltpu.roll(values, 1, 1))
        total = total + jnp.where(z_high, 0.0, pltpu.roll(values, 255, 1))
        total = total + jnp.where(x_low, 0.0, pltpu.roll(values, 1, 0))
        return total + jnp.where(x_high, 0.0, pltpu.roll(values, fine_rows - 1, 0))

    def local_part(real, imag):
        out_real = (
            source_real
            + inner_sum(real)
            - (6.0 * real - wave * (real - shift_imag * imag))
        )
        out_imag = (
            source_imag
            + inner_sum(imag)
            - (6.0 * imag - wave * (imag + shift_imag * real))
        )
        return out_real, out_imag

    links = [[link_ref[slot * 6 + face] for face in range(6)] for slot in range(slots)]
    safe = [[jnp.maximum(link, 0) for link in line] for line in links]
    valid = [[(link >= 0).astype(F32) for link in line] for line in links]
    packed_lane = iota((16, 128), 1) >> 5
    row16 = iota((16, 256), 0)

    def add_ghosts(stage, out_real, out_imag):
        blocks = []
        for slot in range(slots):
            got = [
                faces[stage][safe[slot][face]] * valid[slot][face] for face in range(2, 6)
            ]
            blocks.append(
                jnp.where(
                    packed_lane == 1,
                    got[0],
                    jnp.where(
                        packed_lane == 0,
                        got[1],
                        jnp.where(packed_lane == 3, got[2], got[3]),
                    ),
                )
            )
        spread = times_selector(jnp.concatenate(blocks, 0), unpack)
        result = []
        for part, own in ((0, out_real), (1, out_imag)):
            layers = []
            for slot in range(slots):
                layer = jnp.zeros((16, 256), F32)
                for face, ref, at in ((0, below, 0), (1, above, 15)):
                    link = safe[slot][face]
                    owner = link >> 2
                    first = (link & 3) * 2 + part
                    line = jnp.concatenate(
                        [
                            ref[stage][owner, pl.ds(first, 1), :],
                            ref[stage][owner, pl.ds(first + 8, 1), :],
                        ],
                        1,
                    )
                    layer = jnp.where(row16 == at, line * valid[slot][face], layer)
                layers.append(layer)
            ghosts = jnp.concatenate(layers, 0) + spread[:, part * 256 : part * 256 + 256]
            result.append(own + ghosts)
        return result

    for stage in range(2):
        resid = local_part(real, imag)
        receive(*face_exchange(stage))
        resid_real, resid_imag = add_ghosts(stage, *resid)
        real, imag = (
            real + (resid_real * step_real - resid_imag * step_imag),
            imag + (resid_real * step_imag + resid_imag * step_real),
        )
        put_faces(stage + 1, real, imag)
        send(*face_exchange(stage + 1))

    resid = local_part(real, imag)
    receive(*meta_exchange)
    gathered = n_sub * 8
    meta_row = iota((gathered, 128), 0)
    meta_lane = iota((gathered, 128), 1)
    selectors = []
    coarse = []
    lane = iota((patch_rows, 128), 1)
    patch = iota((patch_rows, 128), 0)
    sign = jnp.where(lane < 64, -1.0, 1.0)

    def placed_of(selector, values):
        terms = jnp.concatenate(terms_of(values, 3), 1)
        product = jnp.dot(selector, terms, preferred_element_type=F32)
        return product[:, :128] + product[:, 128:256] + product[:, 256:]

    for slab in range(3):
        known = meta[slab].reshape(gathered, 128)
        names = pltpu.roll(known, gathered - slots, 0)
        chosen = ((meta_row & 7) < slots) & (names == (meta_lane + 1).astype(F32))
        selector = chosen.astype(F32).T[:patch_rows].astype(BF16)
        selectors.append(selector)
        coarse_wave = placed_of(selector, known)
        diag = 6.0 / 16.0 - coarse_wave
        side = shift_imag * coarse_wave
        factor = omega_coarse / (diag * diag + side * side)
        coarse.append((coarse_wave, diag * factor, side * factor * sign))

    lane512 = iota((512, 128), 1)
    restrict = block_match(iota((512, 128), 0), lane512)
    grow = block_match(iota((128, 512), 1), iota((128, 512), 0))
    fine_lane = iota((fine_rows, 128), 1)
    same_x = ((iota((fine_rows, 128), 0) & 15) >> 2) == ((fine_lane >> 4) & 3)

    receive(*face_exchange(2))
    resid_real, resid_imag = add_ghosts(2, *resid)
    sums = times_selector(jnp.concatenate([resid_real, resid_imag], 1), restrict)
    sums = jnp.where(same_x, sums, 0.0) * (1.0 / 64.0)
    lines = [
        jnp.sum(sums[slot * 16 : slot * 16 + 16], axis=0, keepdims=True) for slot in range(slots)
    ]
    lines.append(jnp.zeros((8 - slots, 128), F32))
    rows[1, s] = jnp.concatenate(lines, 0)
    send(*coarse_exchange)

    lane_x = (lane >> 4) & 3
    lane_y = (lane >> 2) & 3
    lane_z = lane & 3
    patch_y = patch >> 2
    patch_z = patch & 3
    y_first = patch_y == 0
    y_last = patch_y >= rows_y - 1
    z_first = patch_z == 0
    z_last = patch_z == PZ - 1

    def turned(values, shift):
        return pltpu.roll(values, shift % 128, 1)

    def moved(values, shift):
        return pltpu.roll(values, shift % patch_rows, 0)

    def across(values, shift, outside):
        return jnp.where(outside, 0.0, moved(values, shift))

    def coarse_sum(lower, values, upper):
        x_down = turned(values, 16)
        x_up = turned(values, -16)
        edge = jnp.zeros_like(values) if lower is None else turned(lower, -48)
        total = jnp.where(lane_x == 0, edge, x_down)
        edge = jnp.zeros_like(values) if upper is None else turned(upper, 48)
        total = total + jnp.where(lane_x == 3, edge, x_up)
        total = total + jnp.where(
            lane_y == 0, turned(across(values, PZ, y_first), -12), turned(values, 4)
        )
        total = total + jnp.where(
            lane_y == 3, turned(across(values, -PZ, y_last), 12), turned(values, -4)
        )
        total = total + jnp.where(
            lane_z == 0, turned(across(values, 1, z_first), -3), turned(values, 1)
        )
        return total + jnp.where(
            lane_z == 3, turned(across(values, -1, z_last), 3), turned(values, -1)
        )

    def coarse_step(slab, values):
        _, near, cross = coarse[slab]
        return values * near + turned(values, 64) * cross

    receive(*coarse_exchange)
    right = [
        placed_of(selectors[slab], rows[slab].reshape(gathered, 128)) for slab in range(3)
    ]
    there = [has_low.astype(F32), None, has_high.astype(F32)]

    def kept(slab, values):
        return values if there[slab] is None else values * there[slab]

    errors = [kept(slab, coarse_step(slab, right[slab])) for slab in range(3)]
    for sweep in range(CITER - 1):
        following = list(errors)
        for slab in (0, 1, 2) if sweep < CITER - 2 else (1,):
            values = errors[slab]
            lower = errors[slab - 1] if slab > 0 else None
            upper = errors[slab + 1] if slab < 2 else None
            coarse_wave = coarse[slab][0]
            applied = (6.0 * values - coarse_sum(lower, values, upper)) * (1.0 / 16.0)
            applied = applied - coarse_wave * (
                values + shift_imag * sign * turned(values, 64)
            )
            following[slab] = kept(
                slab, values + coarse_step(slab, right[slab] - applied)
            )
        errors = following

    placed_e[...] = errors[1]
    grown = []
    for slot in range(slots):
        line = placed_e[pl.ds(jnp.maximum(patch_of[slot], 0), 1), :]
        grown.append(jnp.broadcast_to(line, (16, 128)))
    grown = jnp.where(same_x, jnp.concatenate(grown, 0), 0.0)
    grown = times_selector(grown, grow)
    for slot in range(slots):
        live = patch_of[slot] >= 0
        span = slice(slot * 16, slot * 16 + 16)
        out_ref[slot, 0] = jnp.where(live, real[span] + grown[span, :256], 0.0)
        out_ref[slot, 1] = jnp.where(live, imag[span] + grown[span, 256:], 0.0)

    for stage in range(ROUNDS):
        sent(*face_exchange(stage))
    sent(*meta_exchange)
    sent(*coarse_exchange)


def body(n_grp, n_sub, field, source, patch_of_slot, neighbour, wave_index, wave_table):
    slots = field.shape[0]
    patch_rows = -(-3 * n_sub // 8) * 8
    stages = ROUNDS + 2
    smem = pl.BlockSpec(memory_space=pltpu.SMEM)
    vmem = pl.BlockSpec(memory_space=pltpu.VMEM)
    dma = pltpu.SemaphoreType.DMA((stages, n_sub))
    return pl.pallas_call(
        functools.partial(kernel, n_grp, n_sub),
        out_shape=jax.ShapeDtypeStruct(field.shape, F32),
        in_specs=[smem] * 4 + [vmem] * 2,
        out_specs=vmem,
        scratch_shapes=[pltpu.VMEM((n_sub * slots, 16, 128), F32)] * ROUNDS
        + [pltpu.VMEM((n_sub, 4 * slots, 128), F32)] * (2 * ROUNDS)
        + [
            pltpu.VMEM((ROUNDS, 2, 4 * slots, 128), F32),
            pltpu.VMEM((3, n_sub, 8, 128), F32),
            pltpu.VMEM((3, n_sub, 8, 128), F32),
            pltpu.VMEM((patch_rows, 128), F32),
        ]
        + [dma] * 6,
        compiler_params=pltpu.CompilerParams(
            collective_id=0, has_side_effects=True, vmem_limit_bytes=24 * 1024 * 1024
        ),
    )(
        patch_of_slot,
        neighbour.reshape(-1),
        wave_index,
        wave_table,
        field,
        source,
    )


def solution(mesh):
    return jax.shard_map(
        functools.partial(body, mesh.shape["grp"], mesh.shape["sub"]),
        mesh=mesh,
        in_specs=(
            P(("grp", "sub"), None, None, None),
            P(("grp", "sub"), None, None, None),
            P(("grp", "sub")),
            P(("grp", "sub"), None),
            P(("grp", "sub")),
            P(),
        ),
        out_specs=P(("grp", "sub"), None, None, None),
        check_vma=False,
    )
```

time: 174 us -> 26.8 us (0.15)
  local copies, waits for them, and re-layouts: 74.1 us -> 3.28 us
  blocking collectives: 30.1 us -> 0 us
  starting transfers between devices: 28.8 us -> 0 us
  other arithmetic: 24.2 us -> 0 us
  Pallas kernels: 0 us -> 23.3 us
  waiting for transfers between devices: 13.9 us -> 0 us
  between operations: 1.96 us -> 0.02 us
    ppermute x10 -> x0, starting transfers between devices: 28.8 us -> none  [the longest x5 21.7 us: padded_2(): lax.ppermute(tail, axis, [(i, (i + 1) % count) for i in range(ends)])]
    slice x29 -> x0, local copies, waits for them, and re-layouts: 28 us -> none  [the longest x5 6.13 us: faces_of(): cubes[:, :, :, -1]]
    pallas_call x0 -> x1, Pallas kernels: none -> 23.3 us  [body(): pl.pallas_call(functools.partial(kernel, n_grp, n_sub), out_shape=jax.Sha...]
    all_gather x4 -> x0, blocking collectives: 23.2 us -> none  [the longest x3 18.1 us: ghost_layers(): table = lax.all_gather(own_faces, 'sub', axis=0, tiled=True)]
    another operation x53 -> x0, local copies, waits for them, and re-layouts: 18.8 us -> none  [the longest x3 5.84 us: neighbour_sum(): ghost_sheets[:, 3][:, :, :, None]]
    ppermute x10 -> x0, waiting for transfers between devices: 13.9 us -> none  [the longest x5 13.9 us: padded_2(): lax.ppermute(head, axis, [((i + 1) % count, i) for i in range(ends)])]
    add x8 -> x0, other arithmetic: 13.7 us -> none  [the longest x3 12.2 us: neighbour_sum(): total + jnp.concatenate([cubes[..., 1:], ghost_sheets[:, 5][..., None]], 4)]
    reshape x9 -> x1, local copies, waits for them, and re-layouts: 9.44 us -> 0.8 us  [body(): neighbour.reshape(-1)]
  transfers between devices with their start and end apart: 10 -> 0, of which waited for: 4 -> 0; matrix products, arithmetic and copies ran while one was open for 13% -> 0% of each run, Pallas kernels for 0% -> 0%
where the time goes in v1:
time: 26.8 us; the launch traced here: 26.6 us
  Pallas kernels  23.3 us (87%)
  local copies, waits for them, and re-layouts  3.28 us (12%)
    pallas_call x1, Pallas kernels, body(): pl.pallas_call(functools.partial(kernel, n_grp, n_sub), out_shape=jax.Sha...  23.3 us
    unnamed x11, local copies, waits for them, and re-layouts  2.47 us
    reshape x1, local copies, waits for them, and re-layouts, body(): neighbour.reshape(-1)  0.8 us

profile of v1, /device:TPU:0, one launch (start us, length us, event | category | flops | bytes accessed | tf_op | source)
XLA Modules:
  0.0 26.6 jit_solution(2545158165031267733)
XLA Ops:
  0.0 0.0 copy-start.4
  0.0 0.0 copy-start.3
  0.0 0.0 copy-start.2
  0.0 0.8 %reshape.3.link_ref = s32[24]{0:T(128)S(1)} reshape(s32[4,6]{1,0:T(4,128)} %param.9) | data formatting | bytes 192 | tf_op jit(solution)/shard_map/reshape | solution.py:555
  0.8 0.0 copy-done.4
  0.8 0.0 copy-done.3
  0.8 0.0 copy-done.2
  0.8 0.0 copy-start
  0.8 0.9 %copy-done = f32[4,2,16,256]{3,2,1,0:T(8,128)S(1)} copy-done((f32[4,2,16,256]{3,2,1,0:T(8,128)S(1)}, f32[4,2,16,256]{3,2,1,0:T(8,128)}, u32[]{:S(2)}) %copy-start) | copy-done | bytes 131096
  1.7 0.0 copy-start.1
  1.7 0.9 %copy-done.1 = f32[4,2,16,256]{3,2,1,0:T(8,128)S(1)} copy-done((f32[4,2,16,256]{3,2,1,0:T(8,128)S(1)}, f32[4,2,16,256]{3,2,1,0:T(8,128)}, u32[]{:S(2)}) %copy-start.1) | copy-done | bytes 131096
  2.6 23.3 %shard_map.64 = f32[4,2,16,256]{3,2,1,0:T(8,128)S(1)} custom-call(s32[4]{0:T(128)S(1)} %copy-done.2, s32[24]{0:T(128)S(1)} %reshape.3.link_ref, s32[4]{0:T(128)S(1)} %copy-done.3, f32[16]{0:T(128)S(1)} %copy-done.4, f32[4,2,16,256]{3,2,1,0:T(8,128)S(1)} %copy-done, f32[4,2,16,256]{3,2,1,0:T(8,128)S(1)} %copy-done.1), custom_call_target="tpu_custom_call" | custom-call | tf_op jit(solution)/shard_map/pallas_call | solution.py:536
  26.0 0.7 %copy.8 = f32[4,2,16,256]{3,2,1,0:T(8,128)} copy(f32[4,2,16,256]{3,2,1,0:T(8,128)S(1)} %shard_map.64) | data formatting | bytes 262144
Async XLA Ops:
  0.0 0.8 %copy-start.4 = (f32[16]{0:T(128)S(1)}, f32[16]{0:T(128)}, u32[]{:S(2)}) copy-start(f32[16]{0:T(128)} %table_ref.1) | copy-start | bytes 196
  0.0 0.8 %copy-start.3 = (s32[4]{0:T(128)S(1)}, s32[4]{0:T(128)}, u32[]{:S(2)}) copy-start(s32[4]{0:T(128)} %index_ref.1) | copy-start | bytes 52
  0.0 0.8 %copy-start.2 = (s32[4]{0:T(128)S(1)}, s32[4]{0:T(128)}, u32[]{:S(2)}) copy-start(s32[4]{0:T(128)} %patch_ref.1) | copy-start | bytes 52
  0.8 0.9 %copy-start = (f32[4,2,16,256]{3,2,1,0:T(8,128)S(1)}, f32[4,2,16,256]{3,2,1,0:T(8,128)}, u32[]{:S(2)}) copy-start(f32[4,2,16,256]{3,2,1,0:T(8,128)} %field_ref.1) | copy-start | bytes 393220
  1.7 0.9 %copy-start.1 = (f32[4,2,16,256]{3,2,1,0:T(8,128)S(1)}, f32[4,2,16,256]{3,2,1,0:T(8,128)}, u32[]{:S(2)}) copy-start(f32[4,2,16,256]{3,2,1,0:T(8,128)} %source_ref.1) | copy-start | bytes 393220

commit v2 on v1

--- a/solution.py
+++ b/solution.py
@@ -84,9 +84,12 @@
     link_ref,
     index_ref,
     table_ref,
+    field_in,
+    source_in,
+    out_ref,
     field_ref,
     source_ref,
-    out_ref,
+    input_sem,
     faces_0,
     faces_1,
     faces_2,
@@ -126,6 +129,11 @@
     def before(step):
         return lax.rem(s + n_sub - step, n_sub)
 
+    field_copy = pltpu.make_async_copy(field_in, field_ref, input_sem.at[0])
+    source_copy = pltpu.make_async_copy(source_in, source_ref, input_sem.at[1])
+    field_copy.start()
+    source_copy.start()
+
     barrier = pltpu.get_barrier_semaphore()
     for step in range(1, n_sub):
         pl.semaphore_signal(barrier, inc=1, device_id=(g, beside(step)), device_id_type=MESH)
@@ -175,7 +183,11 @@
             device_id_type=MESH,
         )
 
-    def send(stage, slab_of, low_src, low_of, high_src, high_of):
+    def send_slab(stage, slab_of, *_):
+        for step in range(1, n_sub):
+            slab_copy(slab_of, stage, step, s).start()
+
+    def send_across(stage, slab_of, low_src, low_of, high_src, high_of):
         @pl.when(has_high)
         def _():
             for step in range(n_sub):
@@ -186,13 +198,11 @@
             for step in range(n_sub):
                 low_copy(low_src, high_of(s), stage, step).start()
 
-        for step in range(1, n_sub):
-            slab_copy(slab_of, stage, step, s).start()
-
-    def receive(stage, slab_of, low_src, low_of, high_src, high_of):
+    def receive_slab(stage, slab_of, *_):
         for step in range(1, n_sub):
             slab_copy(slab_of, stage, step, before(step)).wait_recv()
 
+    def receive_across(stage, slab_of, low_src, low_of, high_src, high_of):
         @pl.when(has_low)
         def _():
             for step in range(n_sub):
@@ -270,15 +280,12 @@
     def joined(ref, part):
         return jnp.concatenate([ref[slot, part] for slot in range(slots)], 0)
 
+    pack = pack_matrix()
+    field_copy.wait()
     real = joined(field_ref, 0)
     imag = joined(field_ref, 1)
 
-    pack = pack_matrix()
-
-    def put_faces(stage, real, imag):
-        packed = times_selector(jnp.concatenate([real, imag], 1), pack)
-        for slot in range(slots):
-            faces[stage][s * slots + slot] = packed[slot * 16 : slot * 16 + 16]
+    def put_sheets(stage, real, imag):
         for side, edge_row in ((0, 0), (1, 15)):
             lines = []
             for half in range(2):
@@ -288,14 +295,23 @@
                         lines.append(values[row : row + 1, half * 128 : half * 128 + 128])
             sheets[stage, side] = jnp.concatenate(lines, 0)
 
+    def put_faces(stage, real, imag):
+        packed = times_selector(jnp.concatenate([real, imag], 1), pack)
+        for slot in range(slots):
+            faces[stage][s * slots + slot] = packed[slot * 16 : slot * 16 + 16]
+
+    put_sheets(0, real, imag)
     put_faces(0, real, imag)
 
     greeted = n_sub - 1 + n_sub * (has_low.astype(jnp.int32) + has_high.astype(jnp.int32))
     pl.semaphore_wait(barrier, greeted)
 
-    send(*face_exchange(0))
-    send(*meta_exchange)
-
+    send_slab(*face_exchange(0))
+    send_across(*face_exchange(0))
+    send_slab(*meta_exchange)
+    send_across(*meta_exchange)
+
+    source_copy.wait()
     source_real = joined(source_ref, 0)
     source_imag = joined(source_ref, 1)
     unpack = unpack_matrix()
@@ -336,13 +352,14 @@
         )
         return out_real, out_imag
 
-    links = [[link_ref[slot * 6 + face] for face in range(6)] for slot in range(slots)]
+    links = [[link_ref[slot, face] for face in range(6)] for slot in range(slots)]
     safe = [[jnp.maximum(link, 0) for link in line] for line in links]
     valid = [[(link >= 0).astype(F32) for link in line] for line in links]
     packed_lane = iota((16, 128), 1) >> 5
     row16 = iota((16, 256), 0)
 
     def add_ghosts(stage, out_real, out_imag):
+        receive_slab(*face_exchange(stage))
         blocks = []
         for slot in range(slots):
             got = [
@@ -360,6 +377,9 @@
                 )
             )
         spread = times_selector(jnp.concatenate(blocks, 0), unpack)
+        out_real = out_real + spread[:, :256]
+        out_imag = out_imag + spread[:, 256:]
+        receive_across(*face_exchange(stage))
         result = []
         for part, own in ((0, out_real), (1, out_imag)):
             layers = []
@@ -378,23 +398,24 @@
                     )
                     layer = jnp.where(row16 == at, line * valid[slot][face], layer)
                 layers.append(layer)
-            ghosts = jnp.concatenate(layers, 0) + spread[:, part * 256 : part * 256 + 256]
-            result.append(own + ghosts)
+            result.append(own + jnp.concatenate(layers, 0))
         return result
 
     for stage in range(2):
         resid = local_part(real, imag)
-        receive(*face_exchange(stage))
         resid_real, resid_imag = add_ghosts(stage, *resid)
         real, imag = (
             real + (resid_real * step_real - resid_imag * step_imag),
             imag + (resid_real * step_imag + resid_imag * step_real),
         )
+        put_sheets(stage + 1, real, imag)
+        send_across(*face_exchange(stage + 1))
         put_faces(stage + 1, real, imag)
-        send(*face_exchange(stage + 1))
+        send_slab(*face_exchange(stage + 1))
 
     resid = local_part(real, imag)
-    receive(*meta_exchange)
+    receive_slab(*meta_exchange)
+    receive_across(*meta_exchange)
     gathered = n_sub * 8
     meta_row = iota((gathered, 128), 0)
     meta_lane = iota((gathered, 128), 1)
@@ -427,7 +448,6 @@
     fine_lane = iota((fine_rows, 128), 1)
     same_x = ((iota((fine_rows, 128), 0) & 15) >> 2) == ((fine_lane >> 4) & 3)
 
-    receive(*face_exchange(2))
     resid_real, resid_imag = add_ghosts(2, *resid)
     sums = times_selector(jnp.concatenate([resid_real, resid_imag], 1), restrict)
     sums = jnp.where(same_x, sums, 0.0) * (1.0 / 64.0)
@@ -436,7 +456,8 @@
     ]
     lines.append(jnp.zeros((8 - slots, 128), F32))
     rows[1, s] = jnp.concatenate(lines, 0)
-    send(*coarse_exchange)
+    send_across(*coarse_exchange)
+    send_slab(*coarse_exchange)
 
     lane_x = (lane >> 4) & 3
     lane_y = (lane >> 2) & 3
@@ -481,7 +502,8 @@
         _, near, cross = coarse[slab]
         return values * near + turned(values, 64) * cross
 
-    receive(*coarse_exchange)
+    receive_slab(*coarse_exchange)
+    receive_across(*coarse_exchange)
     right = [
         placed_of(selectors[slab], rows[slab].reshape(gathered, 128)) for slab in range(3)
     ]
@@ -536,9 +558,11 @@
     return pl.pallas_call(
         functools.partial(kernel, n_grp, n_sub),
         out_shape=jax.ShapeDtypeStruct(field.shape, F32),
-        in_specs=[smem] * 4 + [vmem] * 2,
+        in_specs=[smem] * 4 + [pl.BlockSpec(memory_space=pltpu.HBM)] * 2,
         out_specs=vmem,
-        scratch_shapes=[pltpu.VMEM((n_sub * slots, 16, 128), F32)] * ROUNDS
+        scratch_shapes=[pltpu.VMEM(field.shape, F32)] * 2
+        + [pltpu.SemaphoreType.DMA((2,))]
+        + [pltpu.VMEM((n_sub * slots, 16, 128), F32)] * ROUNDS
         + [pltpu.VMEM((n_sub, 4 * slots, 128), F32)] * (2 * ROUNDS)
         + [
             pltpu.VMEM((ROUNDS, 2, 4 * slots, 128), F32),
@@ -548,11 +572,11 @@
         ]
         + [dma] * 6,
         compiler_params=pltpu.CompilerParams(
-            collective_id=0, has_side_effects=True, vmem_limit_bytes=24 * 1024 * 1024
+            collective_id=0, has_side_effects=True, vmem_limit_bytes=63 * 1024 * 1024
         ),
     )(
         patch_of_slot,
-        neighbour.reshape(-1),
+        neighbour,
         wave_index,
         wave_table,
         field,

time: 26.8 us -> 25.3 us (0.944)
  local copies, waits for them, and re-layouts: 3.28 us -> 1.57 us
  Pallas kernels: 23.3 us -> 23.6 us
    unnamed x11 -> x1, local copies, waits for them, and re-layouts: 2.47 us -> 1.57 us
    reshape x1 -> x0, local copies, waits for them, and re-layouts: 0.8 us -> none  [body(): neighbour.reshape(-1)]
where the time goes in v2:
time: 25.3 us; the launch traced here: 25.2 us
  Pallas kernels  23.6 us (93%)
  local copies, waits for them, and re-layouts  1.57 us (6%)
    pallas_call x1, Pallas kernels, body(): pl.pallas_call(functools.partial(kernel, n_grp, n_sub), out_shape=jax.Sha...  23.6 us
    unnamed x1, local copies, waits for them, and re-layouts  1.57 us

profile of v2, /device:TPU:0, one launch (start us, length us, event | category | flops | bytes accessed | tf_op | source)
XLA Modules:
  0.0 25.2 jit_solution(18269584446593235388)
XLA Ops:
  0.0 23.6 %shard_map.64 = f32[4,2,16,256]{3,2,1,0:T(8,128)} custom-call(s32[4]{0:T(128)} %patch_ref.1, s32[4,6]{1,0:T(4,128)} %link_ref.1, s32[4]{0:T(128)} %index_ref.1, f32[16]{0:T(128)} %table_ref.1, f32[4,2,16,256]{3,2,1,0:T(8,128)} %field_in.1, f32[4,2,16,256]{3,2,1,0:T(8,128)} %source_in.1), custom_call_target="tpu_custom_call" | custom-call | tf_op jit(solution)/shard_map/pallas_call | solution.py:558
  23.6 1.6 %copy.8 = f32[4,2,16,256]{3,2,1,0:T(8,128)} copy(f32[4,2,16,256]{3,2,1,0:T(8,128)} %shard_map.64) | data formatting | bytes 262144

commit v3 on v2

--- a/solution.py
+++ b/solution.py
@@ -183,6 +183,41 @@
             device_id_type=MESH,
         )
 
+    other = s + 1 - 2 * lax.rem(s, 2)
+
+    def face_copy(stage, owner, to, sem):
+        ref = faces[stage].at[pl.ds(owner * slots, slots)]
+        return pltpu.make_async_remote_copy(
+            src_ref=ref,
+            dst_ref=ref,
+            send_sem=slab_send.at[stage, sem],
+            recv_sem=slab_recv.at[stage, sem],
+            device_id=(g, to),
+            device_id_type=MESH,
+        )
+
+    def send_faces(stage):
+        for step in range(2, n_sub, 2):
+            face_copy(stage, s, beside(step), step).start()
+        face_copy(stage, s, other, 1).start()
+
+    def forward_faces(stage):
+        for step in range(2, n_sub, 2):
+            face_copy(stage, before(step), other, step).wait_recv()
+            face_copy(stage, before(step), other, step + 1).start()
+
+    def receive_faces(stage):
+        face_copy(stage, other, other, 1).wait_recv()
+        for step in range(2, n_sub, 2):
+            owner = lax.rem(other + n_sub - step, n_sub)
+            face_copy(stage, owner, other, step + 1).wait_recv()
+
+    def sent_faces(stage):
+        for step in range(2, n_sub, 2):
+            face_copy(stage, s, beside(step), step).wait_send()
+            face_copy(stage, before(step), other, step + 1).wait_send()
+        face_copy(stage, s, other, 1).wait_send()
+
     def send_slab(stage, slab_of, *_):
         for step in range(1, n_sub):
             slab_copy(slab_of, stage, step, s).start()
@@ -213,10 +248,11 @@
             for step in range(n_sub):
                 low_copy(low_src, high_of(before(step)), stage, step).wait_recv()
 
-    def sent(stage, slab_of, low_src, low_of, high_src, high_of):
+    def sent_slab(stage, slab_of, *_):
         for step in range(1, n_sub):
             slab_copy(slab_of, stage, step, s).wait_send()
 
+    def sent_across(stage, slab_of, low_src, low_of, high_src, high_of):
         @pl.when(has_high)
         def _():
             for step in range(n_sub):
@@ -230,7 +266,7 @@
     def face_exchange(stage):
         return (
             stage,
-            lambda owner: faces[stage].at[pl.ds(owner * slots, slots)],
+            None,
             sheets.at[stage, 0],
             lambda owner: below[stage].at[owner],
             sheets.at[stage, 1],
@@ -306,7 +342,7 @@
     greeted = n_sub - 1 + n_sub * (has_low.astype(jnp.int32) + has_high.astype(jnp.int32))
     pl.semaphore_wait(barrier, greeted)
 
-    send_slab(*face_exchange(0))
+    send_faces(0)
     send_across(*face_exchange(0))
     send_slab(*meta_exchange)
     send_across(*meta_exchange)
@@ -359,7 +395,7 @@
     row16 = iota((16, 256), 0)
 
     def add_ghosts(stage, out_real, out_imag):
-        receive_slab(*face_exchange(stage))
+        receive_faces(stage)
         blocks = []
         for slot in range(slots):
             got = [
@@ -403,17 +439,19 @@
 
     for stage in range(2):
         resid = local_part(real, imag)
+        forward_faces(stage)
         resid_real, resid_imag = add_ghosts(stage, *resid)
         real, imag = (
             real + (resid_real * step_real - resid_imag * step_imag),
             imag + (resid_real * step_imag + resid_imag * step_real),
         )
         put_sheets(stage + 1, real, imag)
+        put_faces(stage + 1, real, imag)
+        send_faces(stage + 1)
         send_across(*face_exchange(stage + 1))
-        put_faces(stage + 1, real, imag)
-        send_slab(*face_exchange(stage + 1))
 
     resid = local_part(real, imag)
+    forward_faces(2)
     receive_slab(*meta_exchange)
     receive_across(*meta_exchange)
     gathered = n_sub * 8
@@ -543,9 +581,11 @@
         out_ref[slot, 1] = jnp.where(live, imag[span] + grown[span, 256:], 0.0)
 
     for stage in range(ROUNDS):
-        sent(*face_exchange(stage))
-    sent(*meta_exchange)
-    sent(*coarse_exchange)
+        sent_faces(stage)
+        sent_across(*face_exchange(stage))
+    for exchange in (meta_exchange, coarse_exchange):
+        sent_slab(*exchange)
+        sent_across(*exchange)
 
 
 def body(n_grp, n_sub, field, source, patch_of_slot, neighbour, wave_index, wave_table):

time: 25.3 us -> 25.5 us (level)
  no operation moved by 1% of the time
where the time goes in v3:
time: 25.5 us; the launch traced here: 25.3 us
  Pallas kernels  23.8 us (93%)
  local copies, waits for them, and re-layouts  1.57 us (6%)
    pallas_call x1, Pallas kernels, body(): pl.pallas_call(functools.partial(kernel, n_grp, n_sub), out_shape=jax.Sha...  23.8 us
    unnamed x1, local copies, waits for them, and re-layouts  1.57 us

profile of v3, /device:TPU:0, one launch (start us, length us, event | category | flops | bytes accessed | tf_op | source)
XLA Modules:
  0.0 25.3 jit_solution(1555303126972109819)
XLA Ops:
  0.0 23.8 %shard_map.64 = f32[4,2,16,256]{3,2,1,0:T(8,128)} custom-call(s32[4]{0:T(128)} %patch_ref.1, s32[4,6]{1,0:T(4,128)} %link_ref.1, s32[4]{0:T(128)} %index_ref.1, f32[16]{0:T(128)} %table_ref.1, f32[4,2,16,256]{3,2,1,0:T(8,128)} %field_in.1, f32[4,2,16,256]{3,2,1,0:T(8,128)} %source_in.1), custom_call_target="tpu_custom_call" | custom-call | tf_op jit(solution)/shard_map/pallas_call | solution.py:598
  23.8 1.6 %copy.8 = f32[4,2,16,256]{3,2,1,0:T(8,128)} copy(f32[4,2,16,256]{3,2,1,0:T(8,128)} %shard_map.64) | data formatting | bytes 262144

commit v4 on v3

--- a/solution.py
+++ b/solution.py
@@ -446,9 +446,9 @@
             imag + (resid_real * step_imag + resid_imag * step_real),
         )
         put_sheets(stage + 1, real, imag)
+        send_across(*face_exchange(stage + 1))
         put_faces(stage + 1, real, imag)
         send_faces(stage + 1)
-        send_across(*face_exchange(stage + 1))
 
     resid = local_part(real, imag)
     forward_faces(2)
@@ -612,15 +612,13 @@
         ]
         + [dma] * 6,
         compiler_params=pltpu.CompilerParams(
-            collective_id=0, has_side_effects=True, vmem_limit_bytes=63 * 1024 * 1024
+            collective_id=0, has_side_effects=True, vmem_limit_bytes=24 * 1024 * 1024
         ),
     )(
-        patch_of_slot,
-        neighbour,
-        wave_index,
-        wave_table,
-        field,
-        source,
+        *(
+            pltpu.with_memory_space_constraint(values, pltpu.HBM)
+            for values in (patch_of_slot, neighbour, wave_index, wave_table, field, source)
+        ),
     )
 
 

time: 25.5 us -> 23.9 us (0.937)
  local copies, waits for them, and re-layouts: 1.57 us -> 0.66 us
  Pallas kernels: 23.8 us -> 23 us
    unnamed x1, local copies, waits for them, and re-layouts: 1.57 us -> 0.66 us
    pallas_call x1, Pallas kernels: 23.8 us -> 23 us  [body(): pl.pallas_call(functools.partial(kernel, n_grp, n_sub), out_shape=jax.Sha...]
where the time goes in v4:
time: 23.9 us; the launch traced here: 23.7 us
  Pallas kernels  23 us (96%)
  local copies, waits for them, and re-layouts  0.66 us (3%)
    pallas_call x1, Pallas kernels, body(): pl.pallas_call(functools.partial(kernel, n_grp, n_sub), out_shape=jax.Sha...  23 us
    unnamed x1, local copies, waits for them, and re-layouts  0.66 us

profile of v4, /device:TPU:0, one launch (start us, length us, event | category | flops | bytes accessed | tf_op | source)
XLA Modules:
  0.0 23.7 jit_solution(5010696349436538430)
XLA Ops:
  0.0 23.0 %shard_map.64 = f32[4,2,16,256]{3,2,1,0:T(8,128)S(1)} custom-call(s32[4]{0:T(128)} %patch_ref.1, s32[4,6]{1,0:T(4,128)} %link_ref.1, s32[4]{0:T(128)} %index_ref.1, f32[16]{0:T(128)} %table_ref.1, f32[4,2,16,256]{3,2,1,0:T(8,128)} %field_in.1, f32[4,2,16,256]{3,2,1,0:T(8,128)} %source_in.1), custom_call_target="tpu_custom_call" | custom-call | tf_op jit(solution)/shard_map/pallas_call | solution.py:598
  23.0 0.7 %copy.8 = f32[4,2,16,256]{3,2,1,0:T(8,128)} copy(f32[4,2,16,256]{3,2,1,0:T(8,128)S(1)} %shard_map.64) | data formatting | bytes 262144

commit v5 on v4

--- a/solution.py
+++ b/solution.py
@@ -218,6 +218,10 @@
             face_copy(stage, before(step), other, step + 1).wait_send()
         face_copy(stage, s, other, 1).wait_send()
 
+    def sent_all(stage):
+        sent_faces(stage)
+        sent_across(*face_exchange(stage))
+
     def send_slab(stage, slab_of, *_):
         for step in range(1, n_sub):
             slab_copy(slab_of, stage, step, s).start()
@@ -440,6 +444,8 @@
     for stage in range(2):
         resid = local_part(real, imag)
         forward_faces(stage)
+        if stage:
+            sent_all(stage - 1)
         resid_real, resid_imag = add_ghosts(stage, *resid)
         real, imag = (
             real + (resid_real * step_real - resid_imag * step_imag),
@@ -452,6 +458,9 @@
 
     resid = local_part(real, imag)
     forward_faces(2)
+    sent_all(1)
+    sent_slab(*meta_exchange)
+    sent_across(*meta_exchange)
     receive_slab(*meta_exchange)
     receive_across(*meta_exchange)
     gathered = n_sub * 8
@@ -496,6 +505,10 @@
     rows[1, s] = jnp.concatenate(lines, 0)
     send_across(*coarse_exchange)
     send_slab(*coarse_exchange)
+
+    sent_all(2)
+    sent_slab(*coarse_exchange)
+    sent_across(*coarse_exchange)
 
     lane_x = (lane >> 4) & 3
     lane_y = (lane >> 2) & 3
@@ -579,13 +592,6 @@
         span = slice(slot * 16, slot * 16 + 16)
         out_ref[slot, 0] = jnp.where(live, real[span] + grown[span, :256], 0.0)
         out_ref[slot, 1] = jnp.where(live, imag[span] + grown[span, 256:], 0.0)
-
-    for stage in range(ROUNDS):
-        sent_faces(stage)
-        sent_across(*face_exchange(stage))
-    for exchange in (meta_exchange, coarse_exchange):
-        sent_slab(*exchange)
-        sent_across(*exchange)
 
 
 def body(n_grp, n_sub, field, source, patch_of_slot, neighbour, wave_index, wave_table):

time: 23.9 us -> 23.8 us (level)
  no operation moved by 1% of the time
where the time goes in v5:
time: 23.8 us; the launch traced here: 23.6 us
  Pallas kernels  23 us (97%)
  local copies, waits for them, and re-layouts  0.66 us (3%)
    pallas_call x1, Pallas kernels, body(): pl.pallas_call(functools.partial(kernel, n_grp, n_sub), out_shape=jax.Sha...  23 us
    unnamed x1, local copies, waits for them, and re-layouts  0.66 us

profile of v5, /device:TPU:0, one launch (start us, length us, event | category | flops | bytes accessed | tf_op | source)
XLA Modules:
  0.0 23.6 jit_solution(7575521360061792953)
XLA Ops:
  0.0 23.0 %shard_map.64 = f32[4,2,16,256]{3,2,1,0:T(8,128)S(1)} custom-call(s32[4]{0:T(128)} %patch_ref.1, s32[4,6]{1,0:T(4,128)} %link_ref.1, s32[4]{0:T(128)} %index_ref.1, f32[16]{0:T(128)} %table_ref.1, f32[4,2,16,256]{3,2,1,0:T(8,128)} %field_in.1, f32[4,2,16,256]{3,2,1,0:T(8,128)} %source_in.1), custom_call_target="tpu_custom_call" | custom-call | tf_op jit(solution)/shard_map/pallas_call | solution.py:604
  23.0 0.7 %copy.8 = f32[4,2,16,256]{3,2,1,0:T(8,128)} copy(f32[4,2,16,256]{3,2,1,0:T(8,128)S(1)} %shard_map.64) | data formatting | bytes 262144

commit v6 on v5

--- a/solution.py
+++ b/solution.py
@@ -218,9 +218,75 @@
             face_copy(stage, before(step), other, step + 1).wait_send()
         face_copy(stage, s, other, 1).wait_send()
 
+    def layer_copy(ref, owner, sends, recvs, stage, sem):
+        return pltpu.make_async_remote_copy(
+            src_ref=ref[stage].at[owner],
+            dst_ref=ref[stage].at[owner],
+            send_sem=sends.at[stage, sem],
+            recv_sem=recvs.at[stage, sem],
+            device_id=(g, other),
+            device_id_type=MESH,
+        )
+
+    def low_layers(owner, stage, sem):
+        return layer_copy(below, owner, low_send, low_recv, stage, sem)
+
+    def high_layers(owner, stage, sem):
+        return layer_copy(above, owner, high_send, high_recv, stage, sem)
+
+    def send_layers(stage):
+        @pl.when(has_high)
+        def _():
+            for step in range(0, n_sub, 2):
+                high_copy(sheets.at[stage, 1], below[stage].at[s], stage, step).start()
+
+        @pl.when(has_low)
+        def _():
+            for step in range(0, n_sub, 2):
+                low_copy(sheets.at[stage, 0], above[stage].at[s], stage, step).start()
+
+    def forward_layers(stage):
+        @pl.when(has_low)
+        def _():
+            for step in range(0, n_sub, 2):
+                low_layers(before(step), stage, step).wait_recv()
+                low_layers(before(step), stage, step + 1).start()
+
+        @pl.when(has_high)
+        def _():
+            for step in range(0, n_sub, 2):
+                high_layers(before(step), stage, step).wait_recv()
+                high_layers(before(step), stage, step + 1).start()
+
+    def receive_layers(stage):
+        @pl.when(has_low)
+        def _():
+            for step in range(0, n_sub, 2):
+                owner = lax.rem(other + n_sub - step, n_sub)
+                low_layers(owner, stage, step + 1).wait_recv()
+
+        @pl.when(has_high)
+        def _():
+            for step in range(0, n_sub, 2):
+                owner = lax.rem(other + n_sub - step, n_sub)
+                high_layers(owner, stage, step + 1).wait_recv()
+
+    def sent_layers(stage):
+        @pl.when(has_high)
+        def _():
+            for step in range(0, n_sub, 2):
+                high_copy(sheets.at[stage, 1], below[stage].at[s], stage, step).wait_send()
+                high_layers(before(step), stage, step + 1).wait_send()
+
+        @pl.when(has_low)
+        def _():
+            for step in range(0, n_sub, 2):
+                low_copy(sheets.at[stage, 0], above[stage].at[s], stage, step).wait_send()
+                low_layers(before(step), stage, step + 1).wait_send()
+
     def sent_all(stage):
         sent_faces(stage)
-        sent_across(*face_exchange(stage))
+        sent_layers(stage)
 
     def send_slab(stage, slab_of, *_):
         for step in range(1, n_sub):
@@ -266,16 +332,6 @@
         def _():
             for step in range(n_sub):
                 low_copy(low_src, high_of(s), stage, step).wait_send()
-
-    def face_exchange(stage):
-        return (
-            stage,
-            None,
-            sheets.at[stage, 0],
-            lambda owner: below[stage].at[owner],
-            sheets.at[stage, 1],
-            lambda owner: above[stage].at[owner],
-        )
 
     def row_exchange(stage, ref):
         mine = ref.at[1, s]
@@ -347,7 +403,7 @@
     pl.semaphore_wait(barrier, greeted)
 
     send_faces(0)
-    send_across(*face_exchange(0))
+    send_layers(0)
     send_slab(*meta_exchange)
     send_across(*meta_exchange)
 
@@ -419,7 +475,7 @@
         spread = times_selector(jnp.concatenate(blocks, 0), unpack)
         out_real = out_real + spread[:, :256]
         out_imag = out_imag + spread[:, 256:]
-        receive_across(*face_exchange(stage))
+        receive_layers(stage)
         result = []
         for part, own in ((0, out_real), (1, out_imag)):
             layers = []
@@ -444,6 +500,7 @@
     for stage in range(2):
         resid = local_part(real, imag)
         forward_faces(stage)
+        forward_layers(stage)
         if stage:
             sent_all(stage - 1)
         resid_real, resid_imag = add_ghosts(stage, *resid)
@@ -452,12 +509,13 @@
             imag + (resid_real * step_imag + resid_imag * step_real),
         )
         put_sheets(stage + 1, real, imag)
-        send_across(*face_exchange(stage + 1))
+        send_layers(stage + 1)
         put_faces(stage + 1, real, imag)
         send_faces(stage + 1)
 
     resid = local_part(real, imag)
     forward_faces(2)
+    forward_layers(2)
     sent_all(1)
     sent_slab(*meta_exchange)
     sent_across(*meta_exchange)

time: 23.8 us -> 24.7 us (1.038)
  Pallas kernels: 23 us -> 23.8 us
    pallas_call x1, Pallas kernels: 23 us -> 23.8 us  [body(): pl.pallas_call(functools.partial(kernel, n_grp, n_sub), out_shape=jax.Sha...]
where the time goes in v6:
time: 24.7 us; the launch traced here: 24.5 us
  Pallas kernels  23.8 us (96%)
  local copies, waits for them, and re-layouts  0.66 us (3%)
    pallas_call x1, Pallas kernels, body(): pl.pallas_call(functools.partial(kernel, n_grp, n_sub), out_shape=jax.Sha...  23.8 us
    unnamed x1, local copies, waits for them, and re-layouts  0.66 us

profile of v6, /device:TPU:0, one launch (start us, length us, event | category | flops | bytes accessed | tf_op | source)
XLA Modules:
  0.0 24.5 jit_solution(17104857788330313988)
XLA Ops:
  0.0 23.8 %shard_map.64 = f32[4,2,16,256]{3,2,1,0:T(8,128)S(1)} custom-call(s32[4]{0:T(128)} %patch_ref.1, s32[4,6]{1,0:T(4,128)} %link_ref.1, s32[4]{0:T(128)} %index_ref.1, f32[16]{0:T(128)} %table_ref.1, f32[4,2,16,256]{3,2,1,0:T(8,128)} %field_in.1, f32[4,2,16,256]{3,2,1,0:T(8,128)} %source_in.1), custom_call_target="tpu_custom_call" | custom-call | tf_op jit(solution)/shard_map/pallas_call | solution.py:662
  23.8 0.7 %copy.8 = f32[4,2,16,256]{3,2,1,0:T(8,128)} copy(f32[4,2,16,256]{3,2,1,0:T(8,128)S(1)} %shard_map.64) | data formatting | bytes 262144

commit v7 on v5

--- a/solution.py
+++ b/solution.py
@@ -183,8 +183,6 @@
             device_id_type=MESH,
         )
 
-    other = s + 1 - 2 * lax.rem(s, 2)
-
     def face_copy(stage, owner, to, sem):
         ref = faces[stage].at[pl.ds(owner * slots, slots)]
         return pltpu.make_async_remote_copy(
@@ -197,26 +195,16 @@
         )
 
     def send_faces(stage):
-        for step in range(2, n_sub, 2):
+        for step in range(1, n_sub):
             face_copy(stage, s, beside(step), step).start()
-        face_copy(stage, s, other, 1).start()
-
-    def forward_faces(stage):
-        for step in range(2, n_sub, 2):
-            face_copy(stage, before(step), other, step).wait_recv()
-            face_copy(stage, before(step), other, step + 1).start()
 
     def receive_faces(stage):
-        face_copy(stage, other, other, 1).wait_recv()
-        for step in range(2, n_sub, 2):
-            owner = lax.rem(other + n_sub - step, n_sub)
-            face_copy(stage, owner, other, step + 1).wait_recv()
+        for step in range(1, n_sub):
+            face_copy(stage, before(step), beside(step), step).wait_recv()
 
     def sent_faces(stage):
-        for step in range(2, n_sub, 2):
+        for step in range(1, n_sub):
             face_copy(stage, s, beside(step), step).wait_send()
-            face_copy(stage, before(step), other, step + 1).wait_send()
-        face_copy(stage, s, other, 1).wait_send()
 
     def sent_all(stage):
         sent_faces(stage)
@@ -443,7 +431,6 @@
 
     for stage in range(2):
         resid = local_part(real, imag)
-        forward_faces(stage)
         if stage:
             sent_all(stage - 1)
         resid_real, resid_imag = add_ghosts(stage, *resid)
@@ -457,7 +444,6 @@
         send_faces(stage + 1)
 
     resid = local_part(real, imag)
-    forward_faces(2)
     sent_all(1)
     sent_slab(*meta_exchange)
     sent_across(*meta_exchange)

time: 23.8 us -> 23.7 us (level)
  no operation moved by 1% of the time
where the time goes in v7:
time: 23.7 us; the launch traced here: 23.6 us
  Pallas kernels  22.9 us (97%)
  local copies, waits for them, and re-layouts  0.66 us (3%)
    pallas_call x1, Pallas kernels, body(): pl.pallas_call(functools.partial(kernel, n_grp, n_sub), out_shape=jax.Sha...  22.9 us
    unnamed x1, local copies, waits for them, and re-layouts  0.66 us

profile of v7, /device:TPU:0, one launch (start us, length us, event | category | flops | bytes accessed | tf_op | source)
XLA Modules:
  0.0 23.6 jit_solution(6372812845793031814)
XLA Ops:
  0.0 22.9 %shard_map.64 = f32[4,2,16,256]{3,2,1,0:T(8,128)S(1)} custom-call(s32[4]{0:T(128)} %patch_ref.1, s32[4,6]{1,0:T(4,128)} %link_ref.1, s32[4]{0:T(128)} %index_ref.1, f32[16]{0:T(128)} %table_ref.1, f32[4,2,16,256]{3,2,1,0:T(8,128)} %field_in.1, f32[4,2,16,256]{3,2,1,0:T(8,128)} %source_in.1), custom_call_target="tpu_custom_call" | custom-call | tf_op jit(solution)/shard_map/pallas_call | solution.py:590
  22.9 0.7 %copy.8 = f32[4,2,16,256]{3,2,1,0:T(8,128)} copy(f32[4,2,16,256]{3,2,1,0:T(8,128)S(1)} %shard_map.64) | data formatting | bytes 262144
